TPU v7x, 32 devices: a whole 2x2x4 slice. The times are simulated.
32 devices in a mesh: tab: 4 (over y, core), row: 8 (over z, x).
Axes of the slice: x: 2, y: 2, z: 4, core: 2. Of those that a mesh axis runs over, the one named last changes fastest.
Arguments:
- ctx_feat: bfloat16 [8, 100, 2048], P('tab', None, 'row'), may hold values from -24 to 24
- qry_feat: bfloat16 [8, 100, 512], P('tab', None, 'row'), may hold values from -24 to 24
- feat_count: int32 [8], P('tab'), may hold values from 3 to 100, as said below
- ctx_count: int32 [8], P('tab'), may hold values from 1024 to 2048, as said below
- qry_count: int32 [8], P('tab'), may hold values from 256 to 512, as said below
- w_emb: bfloat16 [100, 768], replicated, may hold values from -0.625 to 0.625
- ln1_gain: float32 [768], replicated, may hold values from 0.1 to 1.9
- ln1_bias: float32 [768], replicated, may hold values from -3 to 3
- w_qkv: bfloat16 [768, 2304], replicated, may hold values from -0.21875 to 0.21875
- w_out: bfloat16 [768, 768], replicated, may hold values from -6 to 6
- ln2_gain: float32 [768], replicated, may hold values from 0.1 to 1.9
- ln2_bias: float32 [768], replicated, may hold values from -3 to 3
- w_up: bfloat16 [768, 3072], replicated, may hold values from -0.21875 to 0.21875
- b_up: float32 [3072], replicated, may hold values from -3 to 3
- w_down: bfloat16 [3072, 768], replicated, may hold values from -0.109375 to 0.109375
- ctx_cot: bfloat16 [8, 2048, 768], P('tab', 'row'), may hold values from -6 to 6
- qry_cot: bfloat16 [8, 512, 768], P('tab', 'row'), may hold values from -6 to 6
Outputs:
- ctx_out: bfloat16 [8, 2048, 768], P('tab', 'row')
- qry_out: bfloat16 [8, 512, 768], P('tab', 'row')
- ctx_feat_grad: bfloat16 [8, 100, 2048], P('tab', None, 'row')
- qry_feat_grad: bfloat16 [8, 100, 512], P('tab', None, 'row')
- grad_w_emb: float32 [100, 768], replicated
- grad_ln1_gain: float32 [768], P('row')
- grad_ln1_bias: float32 [768], P('row')
- grad_w_qkv: float32 [768, 2304], P('row')
- grad_w_out: float32 [768, 768], P('row')
- grad_ln2_gain: float32 [768], P('row')
- grad_ln2_bias: float32 [768], P('row')
- grad_w_up: float32 [768, 3072], P('row')
- grad_b_up: float32 [3072], P('row')
- grad_w_down: float32 [3072, 768], P('row')
- rms: float32 [4], replicated
Inputs may be any that keep to these rules, and one draw needn't show every extreme that they name: `feat_count`: some table has all 100 slots real. `ctx_count`: among the 2 tables of each index of tab one has all 2048 context rows live. `qry_count`: among the 2 tables of each index of tab one has all 512 query rows live.
All inputs are finite; a program needn't handle non-finite values.
Results may differ from a plain program's by a relative error of at most 0.02.
Values may be sent and summed in bfloat16 or wider, within the bound.
A program may use at most 320 MiB of HBM per device.

v0:
```python
import functools
import math

import jax
import jax.numpy as jnp
from jax import lax
from jax.experimental import pallas as pl
from jax.experimental.pallas import tpu as pltpu
from jax.sharding import PartitionSpec as P

HEAD_DIM = 64


EPS = 1e-05
NEGATIVE = -1e30


def standardize(values):
    center = values - jnp.mean(values, axis=-1, keepdims=True)
    inverse = lax.rsqrt(jnp.mean(center * center, axis=-1, keepdims=True) + EPS)
    return (center * inverse, inverse)


def norm_back(grad_out, normed, inverse, gain):
    scaled = grad_out * gain
    inner = (
        scaled
        - jnp.mean(scaled, axis=-1, keepdims=True)
        - normed * jnp.mean(scaled * normed, axis=-1, keepdims=True)
    )
    grad_gain = jnp.sum(grad_out * normed, axis=(0, 1))
    grad_bias = jnp.sum(grad_out, axis=(0, 1))
    return (inverse * inner, grad_gain, grad_bias)


def gelu_exact(values):
    return jax.nn.gelu(values, approximate=False)


def block_scores(query_heads, key_rows, block_index, block_width, key_count, score_scale):
    table_count, local_rows, head_count, head_size = query_heads.shape
    dmodel = head_count * head_size
    block = lax.dynamic_slice_in_dim(key_rows, block_index * block_width, block_width, 1)
    key_block = block[..., :dmodel].reshape(table_count, block_width, head_count, head_size)
    value_block = block[..., dmodel:].reshape(table_count, block_width, head_count, head_size)
    scores = (
        jnp.einsum("trhe,tkhe->thrk", query_heads, key_block, preferred_element_type=jnp.float32)
        * score_scale
    )
    position = block_index * block_width + jnp.arange(block_width)
    live_keys = position[None, :] < key_count[:, None]
    scores = jnp.where(live_keys[:, None, None, :], scores, NEGATIVE)
    return (scores, key_block, value_block)


def local_by_rows(
    ctx_feat,
    qry_feat,
    feat_count,
    ctx_count,
    qry_count,
    w_emb,
    ln1_gain,
    ln1_bias,
    w_qkv,
    w_out,
    ln2_gain,
    ln2_bias,
    w_up,
    b_up,
    w_down,
    ctx_cot,
    qry_cot,
):
    table_count, slot_count, ctx_rows = ctx_feat.shape
    qry_rows = qry_feat.shape[2]
    local_rows = ctx_rows + qry_rows
    dmodel = w_out.shape[0]
    head_count = dmodel // HEAD_DIM
    score_scale = HEAD_DIM ** (-0.5)
    total_ctx = ctx_rows * lax.axis_size("row")
    row_index = lax.axis_index("row")
    slot_live = (jnp.arange(slot_count)[None, :] < feat_count[:, None]).astype(jnp.bfloat16)
    features = jnp.concatenate([ctx_feat, qry_feat], axis=2) * slot_live[:, :, None]
    ctx_live = (row_index * ctx_rows + jnp.arange(ctx_rows))[None, :] < ctx_count[:, None]
    qry_live = (row_index * qry_rows + jnp.arange(qry_rows))[None, :] < qry_count[:, None]
    valid = jnp.concatenate([ctx_live, qry_live], axis=1).astype(jnp.float32)[..., None]
    embed = jnp.einsum("tfr,fd->trd", features, w_emb, preferred_element_type=jnp.float32)
    normed1, inverse1 = standardize(embed)
    attn_in = (normed1 * ln1_gain + ln1_bias).astype(jnp.bfloat16)
    w_query = w_qkv[:, :dmodel]
    w_pair = w_qkv[:, dmodel:]
    query = jnp.einsum("trd,de->tre", attn_in, w_query, preferred_element_type=jnp.float32).astype(
        jnp.bfloat16
    )
    pairs = jnp.einsum(
        "trd,de->tre", attn_in[:, :ctx_rows], w_pair, preferred_element_type=jnp.float32
    ).astype(jnp.bfloat16)
    gathered = lax.all_gather(pairs, "row", axis=1, tiled=True)
    block_width = math.gcd(total_ctx, 512)
    block_total = total_ctx // block_width
    query_heads = query.reshape(table_count, local_rows, head_count, HEAD_DIM)

    def attend_step(carried, block_index):
        running_max, running_sum, summed = carried
        scores, _, value_block = block_scores(
            query_heads, gathered, block_index, block_width, ctx_count, score_scale
        )
        new_max = jnp.maximum(running_max, jnp.max(scores, axis=-1))
        factor = jnp.exp(running_max - new_max)
        weights = jnp.exp(scores - new_max[..., None])
        running_sum = running_sum * factor + jnp.sum(weights, axis=-1)
        summed = summed * jnp.transpose(factor, (0, 2, 1))[..., None] + jnp.einsum(
            "thrk,tkhe->trhe",
            weights.astype(jnp.bfloat16),
            value_block,
            preferred_element_type=jnp.float32,
        )
        return ((new_max, running_sum, summed), None)

    initial = jnp.full((table_count, head_count, local_rows), NEGATIVE, jnp.float32)
    start_sum = jnp.zeros((table_count, local_rows, head_count, HEAD_DIM), jnp.float32)
    (running_max, running_sum, summed), _ = lax.scan(
        attend_step, (initial, jnp.zeros_like(initial), start_sum), jnp.arange(block_total)
    )
    log_total = running_max + jnp.log(running_sum)
    attended = summed / jnp.transpose(running_sum, (0, 2, 1))[..., None]
    attn_low = attended.reshape(table_count, local_rows, dmodel).astype(jnp.bfloat16)
    branch = jnp.einsum("trd,de->tre", attn_low, w_out, preferred_element_type=jnp.float32)
    mixed = embed + branch
    normed2, inverse2 = standardize(mixed)
    mlp_in = (normed2 * ln2_gain + ln2_bias).astype(jnp.bfloat16)
    hidden = jnp.einsum("trd,de->tre", mlp_in, w_up, preferred_element_type=jnp.float32) + b_up
    activation, gelu_back = jax.vjp(gelu_exact, hidden)
    act_low = activation.astype(jnp.bfloat16)
    mlp = jnp.einsum("tre,ed->trd", act_low, w_down, preferred_element_type=jnp.float32)
    output = (mixed + mlp) * valid
    ctx_out = output[:, :ctx_rows].astype(jnp.bfloat16)
    qry_out = output[:, ctx_rows:].astype(jnp.bfloat16)
    squares = jnp.stack(
        [
            jnp.sum(valid * embed * embed),
            jnp.sum(valid * branch * branch),
            jnp.sum(valid * mlp * mlp),
            jnp.sum(valid * output * output),
        ]
    )
    live_rows = jnp.sum(valid)
    cotangent = jnp.concatenate([ctx_cot, qry_cot], axis=1)
    d_mlp = cotangent * valid.astype(jnp.bfloat16)
    grad_w_down = jnp.einsum("tre,trd->ed", act_low, d_mlp, preferred_element_type=jnp.float32)
    d_act = jnp.einsum("trd,ed->tre", d_mlp, w_down, preferred_element_type=jnp.float32)
    d_hidden = gelu_back(d_act)[0].astype(jnp.bfloat16)
    grad_b_up = jnp.sum(d_hidden.astype(jnp.float32), axis=(0, 1))
    grad_w_up = jnp.einsum("trd,tre->de", mlp_in, d_hidden, preferred_element_type=jnp.float32)
    d_mlp_in = jnp.einsum("tre,de->trd", d_hidden, w_up, preferred_element_type=jnp.float32)
    d_norm2, grad_ln2_gain, grad_ln2_bias = norm_back(d_mlp_in, normed2, inverse2, ln2_gain)
    d_mixed = d_mlp.astype(jnp.float32) + d_norm2
    d_branch = d_mixed.astype(jnp.bfloat16)
    grad_w_out = jnp.einsum("trd,tre->de", attn_low, d_branch, preferred_element_type=jnp.float32)
    d_attn = jnp.einsum("tre,de->trd", d_branch, w_out, preferred_element_type=jnp.float32).astype(
        jnp.bfloat16
    )
    d_attn_heads = d_attn.reshape(table_count, local_rows, head_count, HEAD_DIM)
    dots_rows = jnp.sum(d_attn_heads.astype(jnp.float32) * attended, axis=-1)
    row_dots = jnp.transpose(dots_rows, (0, 2, 1))

    def query_part(block_index):
        scores, key_block, value_block = block_scores(
            query_heads, gathered, block_index, block_width, ctx_count, score_scale
        )
        softened = jnp.exp(scores - log_total[..., None])
        d_soft = jnp.einsum(
            "trhe,tkhe->thrk", d_attn_heads, value_block, preferred_element_type=jnp.float32
        )
        d_scores = (softened * (d_soft - row_dots[..., None])).astype(jnp.bfloat16)
        d_part = (
            jnp.einsum("thrk,tkhe->trhe", d_scores, key_block, preferred_element_type=jnp.float32)
            * score_scale
        )
        return (softened, d_scores, d_part)

    start_query = jnp.zeros((table_count, local_rows, head_count, HEAD_DIM), jnp.float32)

    def grad_step(carried, block_index):
        d_query, d_pairs = carried
        softened, d_scores, d_part = query_part(block_index)
        d_values = jnp.einsum(
            "thrk,trhe->tkhe",
            softened.astype(jnp.bfloat16),
            d_attn_heads,
            preferred_element_type=jnp.float32,
        )
        d_keys = (
            jnp.einsum("thrk,trhe->tkhe", d_scores, query_heads, preferred_element_type=jnp.float32)
            * score_scale
        )
        grad_block = jnp.concatenate(
            [
                d_keys.reshape(table_count, block_width, dmodel),
                d_values.reshape(table_count, block_width, dmodel),
            ],
            axis=-1,
        )
        d_pairs = lax.dynamic_update_slice_in_dim(d_pairs, grad_block, block_index * block_width, 1)
        return ((d_query + d_part, d_pairs), None)

    start_pairs = jnp.zeros((table_count, total_ctx, 2 * dmodel), jnp.float32)
    (d_query, d_pairs), _ = lax.scan(grad_step, (start_query, start_pairs), jnp.arange(block_total))
    own_pairs = lax.psum_scatter(d_pairs, "row", scatter_dimension=1, tiled=True).astype(
        jnp.bfloat16
    )
    d_q = d_query.reshape(table_count, local_rows, dmodel).astype(jnp.bfloat16)
    grad_w_qkv = jnp.concatenate(
        [
            jnp.einsum("trd,tre->de", attn_in, d_q, preferred_element_type=jnp.float32),
            jnp.einsum(
                "trd,tre->de", attn_in[:, :ctx_rows], own_pairs, preferred_element_type=jnp.float32
            ),
        ],
        axis=1,
    )
    d_from_query = jnp.einsum("tre,de->trd", d_q, w_query, preferred_element_type=jnp.float32)
    d_from_pairs = jnp.einsum("tre,de->trd", own_pairs, w_pair, preferred_element_type=jnp.float32)
    d_attn_in = jnp.concatenate(
        [d_from_query[:, :ctx_rows] + d_from_pairs, d_from_query[:, ctx_rows:]], axis=1
    )
    d_norm1, grad_ln1_gain, grad_ln1_bias = norm_back(d_attn_in, normed1, inverse1, ln1_gain)
    d_embed = (d_mixed + d_norm1).astype(jnp.bfloat16)
    grad_w_emb = jnp.einsum("tfr,trd->fd", features, d_embed, preferred_element_type=jnp.float32)
    d_features = jnp.einsum("trd,fd->tfr", d_embed, w_emb, preferred_element_type=jnp.float32)
    d_features = (d_features * slot_live[:, :, None].astype(jnp.float32)).astype(jnp.bfloat16)
    ctx_feat_grad = d_features[:, :, :ctx_rows]
    qry_feat_grad = d_features[:, :, ctx_rows:]
    (
        qkv_part,
        out_part,
        up_part,
        down_part,
        gain1_part,
        bias1_part,
        gain2_part,
        bias2_part,
        upbias_part,
    ) = (
        lax.psum_scatter(grad_w_qkv, "row", scatter_dimension=0, tiled=True),
        lax.psum_scatter(grad_w_out, "row", scatter_dimension=0, tiled=True),
        lax.psum_scatter(grad_w_up, "row", scatter_dimension=0, tiled=True),
        lax.psum_scatter(grad_w_down, "row", scatter_dimension=0, tiled=True),
        lax.psum_scatter(grad_ln1_gain, "row", scatter_dimension=0, tiled=True),
        lax.psum_scatter(grad_ln1_bias, "row", scatter_dimension=0, tiled=True),
        lax.psum_scatter(grad_ln2_gain, "row", scatter_dimension=0, tiled=True),
        lax.psum_scatter(grad_ln2_bias, "row", scatter_dimension=0, tiled=True),
        lax.psum_scatter(grad_b_up, "row", scatter_dimension=0, tiled=True),
    )
    qkv_all, out_all, up_all, down_all, gain1_all, bias1_all, gain2_all, bias2_all, upbias_all = (
        lax.psum(qkv_part.astype(jnp.bfloat16), "tab").astype(jnp.float32),
        lax.psum(out_part.astype(jnp.bfloat16), "tab").astype(jnp.float32),
        lax.psum(up_part.astype(jnp.bfloat16), "tab").astype(jnp.float32),
        lax.psum(down_part.astype(jnp.bfloat16), "tab").astype(jnp.float32),
        lax.psum(gain1_part.astype(jnp.bfloat16), "tab").astype(jnp.float32),
        lax.psum(bias1_part.astype(jnp.bfloat16), "tab").astype(jnp.float32),
        lax.psum(gain2_part.astype(jnp.bfloat16), "tab").astype(jnp.float32),
        lax.psum(bias2_part.astype(jnp.bfloat16), "tab").astype(jnp.float32),
        lax.psum(upbias_part.astype(jnp.bfloat16), "tab").astype(jnp.float32),
    )
    embed_all, squares_all, count_all = lax.psum((grad_w_emb, squares, live_rows), ("tab", "row"))
    rms = jnp.sqrt(squares_all / (count_all * dmodel))
    return (
        ctx_out,
        qry_out,
        ctx_feat_grad,
        qry_feat_grad,
        embed_all,
        gain1_all,
        bias1_all,
        qkv_all,
        out_all,
        gain2_all,
        bias2_all,
        up_all,
        upbias_all,
        down_all,
        rms,
    )


MESH = pl.DeviceIdType.MESH
LANES = 128
NT = (((1,), (1,)), ((), ()))


def lane_of(shape):
    return lax.broadcasted_iota(jnp.int32, shape, len(shape) - 1)


def split_three(values):
    high = values.astype(jnp.bfloat16)
    rest = values - high.astype(jnp.float32)
    mid = rest.astype(jnp.bfloat16)
    tail = (rest - mid.astype(jnp.float32)).astype(jnp.bfloat16)
    return (high, mid, tail)


def set_lanes(values, first, columns):
    lane = lane_of(values.shape)
    values = values.astype(jnp.float32)
    for i, column in enumerate(columns):
        values = jnp.where(lane == first + i, column.astype(jnp.float32), values)
    return values.astype(jnp.bfloat16)


def greet(peers):
    barrier = pltpu.get_barrier_semaphore()
    for peer in peers:
        pl.semaphore_signal(barrier, inc=1, device_id=peer, device_id_type=MESH)
    pl.semaphore_wait(barrier, len(peers))


def front_kernel(
    dims, counts, own_feat, w_emb, gain, bias, w_qkv,
    out_in, queries_out, keys_out, values_out, outs_out, feat_out, w_out,
    feat_in, window, w_lanes, w_mine, queries, keys, values, outs, packed, load_sem, store_sem, send_sem, recv_sem,
):
    row_size, x_size, chunk, ctx_rows, local_rows, heads, groups = dims
    z_size = row_size // x_size
    total = keys.shape[1]
    pair = x_size * local_rows
    dmodel = w_emb.shape[1]
    width = heads * HEAD_DIM
    tab, row = lax.axis_index("tab"), lax.axis_index("row")
    z = row // x_size
    table, group = row // groups, lax.rem(row, groups)
    row_peers = [(tab, lax.rem(row + k, row_size)) for k in range(1, row_size)]
    numbers = {}

    def remote(name, src, dst, peer):
        i = numbers.setdefault(name, len(numbers))
        return pltpu.make_async_remote_copy(
            src_ref=src, dst_ref=dst, send_sem=send_sem.at[i], recv_sem=recv_sem.at[i],
            device_id=peer, device_id_type=MESH,
        )

    def feat_copy(k):
        peer = row_peers[k]
        return remote(("feat", k), own_feat.at[peer[1] // groups], feat_in.at[row], peer)

    def out_copy(shift):
        p = lax.rem(row + shift, row_size)
        return remote(("out", shift), packed.at[p], out_in.at[row], (tab, p))

    span = window.shape[2]
    first = (group * width) // LANES * LANES

    def window_copy(n):
        at = pl.ds(pl.multiple_of(n * dmodel + first, LANES), span)
        return pltpu.make_async_copy(w_qkv.at[:, at], window.at[n], load_sem.at[n])

    for n in range(3):
        window_copy(n).start()
    greet(row_peers)
    for k in range(row_size - 1):
        feat_copy(k).start()
    feat_in[row] = own_feat[table]
    offset = group * width - first
    for n in range(3):
        window_copy(n).wait()
        wide = window[n]
        mine = wide[:, :width]
        for shift in range(HEAD_DIM, span - width + 1, HEAD_DIM):
            mine = jnp.where(offset == shift, wide[:, shift : shift + width], mine)
        w_mine[:, n * width : (n + 1) * width] = mine
        for h in range(heads):
            one = mine[:, h * HEAD_DIM : (h + 1) * HEAD_DIM]
            at = (n * heads + h) * LANES
            w_lanes[:, at : at + LANES] = jnp.concatenate([one, jnp.zeros_like(one)], axis=1)
    w_store = pltpu.make_async_copy(w_mine, w_out, store_sem.at[0])
    w_store.start()
    count = counts[table]

    def project(step, _):
        there = lax.rem(z + step, z_size)
        embeds = []
        for other in range(x_size):
            p = there * x_size + other
            shift = lax.rem(p - row + row_size, row_size)
            for s in range(1, row_size):

                @pl.when(shift == s)
                def _():
                    feat_copy(row_size - s - 1).wait_recv()

            embeds.append(feat_in[p])
        rows_feat = jnp.concatenate(embeds, axis=0)
        embed = jnp.dot(rows_feat, w_emb[...], preferred_element_type=jnp.float32)
        center = embed - jnp.mean(embed, axis=-1, keepdims=True)
        inverse = lax.rsqrt(jnp.mean(center * center, axis=-1, keepdims=True) + EPS)
        attn_in = (center * inverse * gain[...] + bias[...]).astype(jnp.bfloat16)
        projected = jnp.dot(attn_in, w_lanes[...], preferred_element_type=jnp.float32)
        rows = pl.ds(pl.multiple_of(there * pair, LANES), pair)
        lane = lane_of((pair, LANES))
        for h in range(heads):
            query = projected[:, h * LANES : (h + 1) * LANES] * HEAD_DIM ** (-0.5)
            queries[h, rows] = jnp.where(lane == HEAD_DIM, 1.0, query).astype(jnp.bfloat16)
        lane = lane_of((ctx_rows, LANES))
        for other in range(x_size):
            p = there * x_size + other
            key_rows = pl.ds(pl.multiple_of(p * ctx_rows, LANES), ctx_rows)
            position = p * ctx_rows + lax.broadcasted_iota(jnp.int32, (ctx_rows, LANES), 0)
            mask = jnp.where(position < count, 0.0, NEGATIVE)
            for h in range(heads):
                at = (heads + h) * LANES
                key = projected[other * local_rows : other * local_rows + ctx_rows, at : at + LANES]
                key = jnp.where(lane == HEAD_DIM, mask, key)
                key = jnp.where((lane > HEAD_DIM) & (lane < HEAD_DIM + 4), 1.0, key)
                keys[h, key_rows] = key.astype(jnp.bfloat16)
                at = (2 * heads + h) * LANES
                value = projected[other * local_rows : other * local_rows + ctx_rows, at : at + LANES]
                value = jnp.where((lane >= HEAD_DIM) & (lane < HEAD_DIM + 3), 1.0, value)
                values[h, key_rows] = value.astype(jnp.bfloat16)
        return 0

    lax.fori_loop(0, z_size, project, 0)
    stores = [
        pltpu.make_async_copy(src, dst, store_sem.at[i + 1])
        for i, (src, dst) in enumerate(((keys, keys_out), (values, values_out), (feat_in, feat_out)))
    ]
    for store in stores:
        store.start()
    whole = heads // 2

    def segment(step, _):
        k, h = step // heads, lax.rem(step, heads)
        there = lax.rem(z + k + 1, z_size)
        rows = pl.ds(pl.multiple_of(there * pair, LANES), pair)
        query = queries[h, rows]
        for i in range(total // chunk):
            at = pl.ds(i * chunk, chunk)
            scores = lax.dot_general(query, keys[h, at], NT, preferred_element_type=jnp.float32)
            top = jnp.max(scores, axis=-1, keepdims=True)
            if i:
                top = jnp.maximum(top, before)
            weights = jnp.exp(scores - top).astype(jnp.bfloat16)
            term = jnp.dot(weights, values[h, at], preferred_element_type=jnp.float32)
            summed = summed * jnp.exp(before - top) + term if i else term
            before = top
        sum_all = summed[:, HEAD_DIM : HEAD_DIM + 1]
        outs[h, rows] = (summed / sum_all).astype(jnp.bfloat16)
        queries[h, rows] = set_lanes(query, HEAD_DIM + 1, split_three(-(top + jnp.log(sum_all))))

        @pl.when(h == heads - 1)
        def _():
            for other in range(x_size):
                p = there * x_size + other
                at = pl.ds(pl.multiple_of(p * local_rows, 16), local_rows)
                parts = [outs[i, at, :HEAD_DIM] for i in range(heads)]
                for i in range(whole):
                    both = jnp.concatenate([parts[2 * i], parts[2 * i + 1]], axis=1)
                    packed[p, i * local_rows : (i + 1) * local_rows] = both
                if heads % 2:
                    last = parts[-1]
                    both = jnp.concatenate([last[: local_rows // 2], last[local_rows // 2 :]], axis=1)
                    packed[p, whole * local_rows :] = both
                ahead = lax.rem(p - row + row_size, row_size)
                for s in range(1, row_size):

                    @pl.when(ahead == s)
                    def _():
                        out_copy(s).start()

        return 0

    lax.fori_loop(0, z_size * heads, segment, 0)
    last = [
        pltpu.make_async_copy(queries, queries_out, store_sem.at[4]),
        pltpu.make_async_copy(outs, outs_out, store_sem.at[5]),
        pltpu.make_async_copy(packed.at[row], out_in.at[row], store_sem.at[6]),
    ]
    for store in last:
        store.start()
    for k in range(row_size - 1):
        feat_copy(k).wait_send()
    for store in [w_store] + stores + last:
        store.wait()
    for s in range(1, row_size):
        out_copy(s).wait()


def front(counts, own_feat, w_emb, gain, bias, w_qkv, total_ctx, heads, groups, chunk, collective_id):
    row_size = lax.axis_size("row")
    _, local_rows, slots = own_feat.shape
    dmodel = w_emb.shape[1]
    ctx_rows = total_ctx // row_size
    width = heads * HEAD_DIM
    x_size = 2
    span = -(-(width + (HEAD_DIM if width % LANES else 0)) // LANES) * LANES
    bf16 = lambda *shape: (shape, jnp.bfloat16)
    by_query, by_key = (heads, row_size * local_rows, LANES), (heads, total_ctx, LANES)
    block = (row_size, -(-heads * local_rows // 2), LANES)
    feat = (row_size, local_rows, slots)
    vmem = pl.BlockSpec(memory_space=pltpu.VMEM)
    anywhere = pl.BlockSpec(memory_space=pl.ANY)
    scratch = [
        feat, (3, dmodel, span), (dmodel, 3 * heads * LANES), (dmodel, 3 * width),
        by_query, by_key, by_key, by_query, block,
    ]
    return pl.pallas_call(
        functools.partial(front_kernel, (row_size, x_size, chunk, ctx_rows, local_rows, heads, groups)),
        out_shape=[
            jax.ShapeDtypeStruct(s, jnp.bfloat16)
            for s in (block, by_query, by_key, by_key, by_query, feat, (dmodel, 3 * width))
        ],
        in_specs=[pl.BlockSpec(memory_space=pltpu.SMEM)] + [vmem] * 4 + [anywhere],
        out_specs=[anywhere] * 7,
        scratch_shapes=[pltpu.VMEM(s, jnp.bfloat16) for s in scratch] + [
            pltpu.SemaphoreType.DMA((3,)),
            pltpu.SemaphoreType.DMA((7,)),
            pltpu.SemaphoreType.DMA((2 * (row_size - 1),)),
            pltpu.SemaphoreType.DMA((2 * (row_size - 1),)),
        ],
        compiler_params=pltpu.CompilerParams(
            collective_id=collective_id, has_side_effects=True, vmem_limit_bytes=60 * 2**20
        ),
        name="front",
    )(counts, own_feat, w_emb, gain, bias, w_qkv)


def gelu_parts(values):
    below = 0.5 + 0.5 * lax.erf(values * math.sqrt(0.5))
    return (below, values * jnp.exp(-0.5 * values * values) * (1.0 / math.sqrt(2.0 * math.pi)))


def middle_kernel(
    dims, ctx_count, qry_count, own_feat, w_emb, gain, bias, b_up, out_in, w_out_hbm, w_up_hbm, w_down_hbm, ctx_cot, qry_cot,
    ctx_out, qry_out, g_in, up_half, down_half, out_half, d_branch_out, vectors, sums,
    w_out, w_up, w_down, attn_in, cot, attn_low, mlp_in, mlp_in_t, mixed, normed, d_mlp_in, act, d_hidden, d_up_bias,
    packed, up, down, out, up_in0, down_in0, out_in0, load_sem, store_sem, send_sem, recv_sem,
):
    row_size, ctx_rows, local_rows, tables, groups, heads, tile = dims
    rows = tables * local_rows
    qry_rows = local_rows - ctx_rows
    dmodel, hidden_size = w_up.shape
    tiles = hidden_size // tile
    tab, row = lax.axis_index("tab"), lax.axis_index("row")
    core = lax.rem(tab, 2)
    core_peer = (tab ^ 1, row)
    row_peers = [(tab, lax.rem(row + k, row_size)) for k in range(1, row_size)]
    numbers = {}

    def remote(name, src, dst, peer):
        i = numbers.setdefault(name, len(numbers))
        return pltpu.make_async_remote_copy(
            src_ref=src, dst_ref=dst, send_sem=send_sem.at[i], recv_sem=recv_sem.at[i],
            device_id=peer, device_id_type=MESH,
        )

    loads = [
        pltpu.make_async_copy(src, dst, load_sem.at[i])
        for i, (src, dst) in enumerate(
            [(out_in, attn_in), (w_out_hbm, w_out), (w_up_hbm, w_up), (w_down_hbm, w_down)]
            + [(ctx_cot.at[t], cot.at[pl.ds(t * local_rows, ctx_rows)]) for t in range(tables)]
            + [(qry_cot.at[t], cot.at[pl.ds(t * local_rows + ctx_rows, qry_rows)]) for t in range(tables)]
        )
    ]
    for load in loads:
        load.start()
    greet([core_peer] + row_peers)

    at = lax.broadcasted_iota(jnp.int32, (local_rows, 1), 0)
    live = []
    for t in range(tables):
        place = jnp.where(at < ctx_rows, row * ctx_rows + at, row * qry_rows + at - ctx_rows)
        limit = jnp.where(at < ctx_rows, ctx_count[t], qry_count[t])
        live.append(jnp.where(place < limit, 1.0, 0.0))
    valid = jnp.concatenate(live, axis=0)
    own_rows = jnp.concatenate([own_feat[t] for t in range(tables)], axis=0)
    embed = jnp.dot(own_rows, w_emb[...], preferred_element_type=jnp.float32)

    whole = heads // 2
    loads[0].wait()
    for t in range(tables):
        parts = []
        for g in range(groups):
            block = attn_in[t * groups + g]
            for h in range(whole):
                parts.append(block[h * local_rows : (h + 1) * local_rows])
            if heads % 2:
                last = block[whole * local_rows :]
                parts.append(jnp.concatenate([last[:, :HEAD_DIM], last[:, HEAD_DIM:]], axis=0))
        attn_low[t * local_rows : (t + 1) * local_rows] = jnp.concatenate(parts, axis=1)
    loads[1].wait()
    branch = jnp.dot(attn_low[...], w_out[...], preferred_element_type=jnp.float32)
    summed = embed + branch
    mixed[...] = summed
    square_embed = jnp.sum(valid * embed * embed)
    square_branch = jnp.sum(valid * branch * branch)
    center = summed - jnp.mean(summed, axis=-1, keepdims=True)
    inverse = lax.rsqrt(jnp.mean(center * center, axis=-1, keepdims=True) + EPS)
    normed[...] = center * inverse
    mlp_in[...] = (normed[...] * gain[...] + bias[...]).astype(jnp.bfloat16)
    for load in loads[2:]:
        load.wait()
    cot[...] = (cot[...].astype(jnp.float32) * valid).astype(jnp.bfloat16)
    d_mlp_in[...] = jnp.zeros_like(d_mlp_in)

    def columns(i):
        return pl.ds(pl.multiple_of(i * tile, LANES), tile)

    def first(i, _):
        at = columns(i)
        hidden = jnp.dot(mlp_in[...], w_up[:, at], preferred_element_type=jnp.float32) + b_up[:, at]
        d_act = lax.dot_general(cot[...], w_down[at], NT, preferred_element_type=jnp.float32)
        below, slope = gelu_parts(hidden)
        act[:, at] = (hidden * below).astype(jnp.bfloat16)
        grad = (d_act * (below + slope)).astype(jnp.bfloat16)
        d_hidden[:, at] = grad
        d_up_bias[:, at] = jnp.sum(grad.astype(jnp.float32), axis=0, keepdims=True)
        d_mlp_in[...] += lax.dot_general(grad, w_up[:, at], NT, preferred_element_type=jnp.float32)
        return 0

    lax.fori_loop(0, tiles, first, 0)
    grad_in = d_mlp_in[...]
    scaled = grad_in * gain[...]
    inner = (
        scaled
        - jnp.mean(scaled, axis=-1, keepdims=True)
        - normed[...] * jnp.mean(scaled * normed[...], axis=-1, keepdims=True)
    )
    vectors[...] = jnp.zeros_like(vectors)
    vectors[2:3] = jnp.sum(grad_in * normed[...], axis=0, keepdims=True)
    vectors[3:4] = jnp.sum(grad_in, axis=0, keepdims=True)
    for i in range(hidden_size // dmodel):
        vectors[4 + i : 5 + i] = d_up_bias[:, i * dmodel : (i + 1) * dmodel]
    d_branch = (cot[...].astype(jnp.float32) + inverse * inner).astype(jnp.bfloat16)
    for t in range(tables):
        d_branch_out[t] = d_branch[t * local_rows : (t + 1) * local_rows]
    d_attn = lax.dot_general(d_branch, w_out[...], NT, preferred_element_type=jnp.float32).astype(jnp.bfloat16)
    width = heads * HEAD_DIM
    for t in range(tables):
        for g in range(groups):
            block = d_attn[t * local_rows : (t + 1) * local_rows, g * width : (g + 1) * width]
            p = t * groups + g
            for h in range(whole):
                packed[p, h * local_rows : (h + 1) * local_rows] = block[:, h * LANES : (h + 1) * LANES]
            if heads % 2:
                last = block[:, whole * LANES :]
                both = jnp.concatenate([last[: local_rows // 2], last[local_rows // 2 :]], axis=1)
                packed[p, whole * local_rows :] = both
    own_g = pltpu.make_async_copy(packed.at[row], g_in.at[row], store_sem.at[0])
    own_g.start()
    g_copies = [remote(("g", k), packed.at[peer[1]], g_in.at[row], peer) for k, peer in enumerate(row_peers)]
    for copy in g_copies:
        copy.start()

    def half(ref, which):
        size = ref.shape[1] // 2
        return pl.ds(pl.multiple_of(which * size, 16), size)

    shard = dmodel // row_size
    d_out = jnp.dot(attn_low[...].T, d_branch, preferred_element_type=jnp.float32).astype(jnp.bfloat16)
    for p in range(row_size):
        out[p] = d_out[p * shard : (p + 1) * shard]
    out_copy = remote("out", out.at[:, half(out, 1 - core)], out_in0, core_peer)
    out_copy.start()
    mlp_in_t[...] = mlp_in[...].T
    d_mlp_in[...] = jnp.zeros_like(d_mlp_in)
    per = hidden_size // row_size

    def second(p, _):
        at = pl.ds(pl.multiple_of(p * per, LANES), per)
        piece = act[:, at]
        d_mlp_in[...] += jnp.dot(piece, w_down[at], preferred_element_type=jnp.float32)
        down[p] = jnp.dot(piece.T, cot[...], preferred_element_type=jnp.float32).astype(jnp.bfloat16)
        d_up = jnp.dot(mlp_in_t[...], d_hidden[:, at], preferred_element_type=jnp.float32).astype(jnp.bfloat16)
        for q in range(row_size):
            up[q, :, at] = d_up[q * shard : (q + 1) * shard]
        return 0

    lax.fori_loop(0, row_size, second, 0)
    copies = [
        remote("up", up.at[:, half(up, 1 - core)], up_in0, core_peer),
        remote("down", down.at[:, half(down, 1 - core)], down_in0, core_peer),
    ]
    for copy in copies:
        copy.start()
    mlp = d_mlp_in[...]
    result = (mixed[...] + mlp) * valid
    square_mlp = jnp.sum(valid * mlp * mlp)
    square_result = jnp.sum(result * result)
    low = result.astype(jnp.bfloat16)
    for t in range(tables):
        ctx_out[t] = low[t * local_rows : t * local_rows + ctx_rows]
        qry_out[t] = low[t * local_rows + ctx_rows : (t + 1) * local_rows]
    lane = lane_of(sums.shape)
    parts = (square_embed, square_branch, square_mlp, square_result, jnp.sum(valid))
    total = jnp.zeros(sums.shape, jnp.float32)
    for i, part in enumerate(parts):
        total = jnp.where(lane == i, part, total)
    sums[...] = total
    stores = []
    for i, (copy, mine, taken, result_hbm) in enumerate(
        ((out_copy, out, out_in0, out_half), (copies[1], down, down_in0, down_half), (copies[0], up, up_in0, up_half))
    ):
        copy.wait()

        @pl.loop(0, row_size)
        def _(p):
            taken[p] = taken[p] + mine[p, half(mine, core)]

        store = pltpu.make_async_copy(taken, result_hbm, store_sem.at[i + 1])
        store.start()
        stores.append(store)
    for store in stores + [own_g]:
        store.wait()
    for copy in g_copies:
        copy.wait()


def middle(ctx_count, qry_count, own_feat, w_emb, gain, bias, b_up, out_in, w_out, w_up, w_down, ctx_cot, qry_cot,
           groups, heads, tile, collective_id):
    row_size = lax.axis_size("row")
    tables, local_rows, _ = own_feat.shape
    ctx_rows = ctx_cot.shape[1]
    rows = tables * local_rows
    dmodel, hidden_size = w_up.shape
    shard, per = dmodel // row_size, hidden_size // row_size
    halves = [(row_size, shard // 2, hidden_size), (row_size, per // 2, dmodel), (row_size, shard // 2, dmodel)]
    vmem = pl.BlockSpec(memory_space=pltpu.VMEM)
    smem = pl.BlockSpec(memory_space=pltpu.SMEM)
    anywhere = pl.BlockSpec(memory_space=pl.ANY)
    bf16 = lambda *shape: pltpu.VMEM(shape, jnp.bfloat16)
    f32 = lambda *shape: pltpu.VMEM(shape, jnp.float32)
    sends = row_size - 1 + 3
    return pl.pallas_call(
        functools.partial(middle_kernel, (row_size, ctx_rows, local_rows, tables, groups, heads, tile)),
        out_shape=[jax.ShapeDtypeStruct(s, jnp.bfloat16) for s in (ctx_cot.shape, qry_cot.shape, out_in.shape, *halves)]
        + [jax.ShapeDtypeStruct((tables, local_rows, dmodel), jnp.bfloat16)]
        + [jax.ShapeDtypeStruct((4 + hidden_size // dmodel, dmodel), jnp.float32)]
        + [jax.ShapeDtypeStruct((8, LANES), jnp.float32)],
        in_specs=[smem] * 2 + [vmem] * 5 + [anywhere] * 6,
        out_specs=[vmem] * 2 + [anywhere] * 4 + [vmem] * 3,
        scratch_shapes=[
            bf16(*w_out.shape), bf16(*w_up.shape), bf16(*w_down.shape), bf16(*out_in.shape), bf16(rows, dmodel),
            bf16(rows, dmodel), bf16(rows, dmodel), bf16(dmodel, rows),
            f32(rows, dmodel), f32(rows, dmodel), f32(rows, dmodel),
            bf16(rows, hidden_size), bf16(rows, hidden_size), f32(1, hidden_size),
            bf16(*out_in.shape),
            bf16(row_size, shard, hidden_size), bf16(row_size, per, dmodel), bf16(row_size, shard, dmodel),
            *[bf16(*s) for s in halves],
            pltpu.SemaphoreType.DMA((4 + 2 * tables,)),
            pltpu.SemaphoreType.DMA((4,)),
            pltpu.SemaphoreType.DMA((sends,)),
            pltpu.SemaphoreType.DMA((sends,)),
        ],
        compiler_params=pltpu.CompilerParams(
            collective_id=collective_id, has_side_effects=True, vmem_limit_bytes=62 * 2**20
        ),
        name="middle",
    )(ctx_count, qry_count, own_feat, w_emb, gain, bias, b_up, out_in, w_out, w_up, w_down, ctx_cot, qry_cot)


def tile_sum(parts):
    total = parts[0]
    for part in parts[1:]:
        total = total + part
    return total


def back_kernel(
    dims, counts, up0, down0, out0, queries_hbm, keys_hbm, values_hbm, outs_hbm, g_in, feat, w_emb, w_mine, gain, bias,
    own_feat, d_branch, vectors, sums,
    ctx_grad, qry_grad, emb_all, sums_all, qkv_all, out_all, up_all, down_all,
    queries, keys, values, outs, up_own, down_own, out_own, up1, down1, out1, up2, down2, out2,
    up3, down3, out3, up4, down4, out4, grads, d_q, d_kt, d_vt, d_k, d_v, terms, terms_in, d_qkv, d_emb, d_gain, d_bias,
    qkv_own, emb_own, qkv_in0, emb_in0, sums_in0, sums0, qkv_in1, emb_in1, sums_in1,
    qkv1, emb1, sums1, qkv_in2, emb_in2, sums_in2, qkv2, emb2, emb3,
    load_sem, send_sem, recv_sem,
):
    row_size, x_size, chunk, ctx_rows, local_rows = dims
    z_size = row_size // x_size
    heads, total, _ = keys.shape
    pair = x_size * local_rows
    tab, row = lax.axis_index("tab"), lax.axis_index("row")
    core, y = lax.rem(tab, 2), tab // 2
    x, z = lax.rem(row, x_size), row // x_size
    core_peer, y_peer, x_peer = (tab ^ 1, row), (tab ^ 2, row), (tab, row ^ 1)
    row_peers = [(tab, lax.rem(row + k, row_size)) for k in range(1, row_size)]
    z_peers = [(tab, lax.rem(z + k, z_size) * x_size + x) for k in range(1, z_size)]
    numbers = {}

    def remote(name, src, dst, peer):
        i = numbers.setdefault(name, len(numbers))
        return pltpu.make_async_remote_copy(
            src_ref=src, dst_ref=dst, send_sem=send_sem.at[i], recv_sem=recv_sem.at[i],
            device_id=peer, device_id_type=MESH,
        )

    def half(rows, which):
        return pl.ds(pl.multiple_of(which * (rows // 2), 16), rows // 2)

    def columns(ref, which):
        wide = ref.shape[-1] // 2
        return pl.ds(pl.multiple_of(which * wide, LANES), wide)

    def by_z(ref):
        return ref.reshape(z_size, x_size, *ref.shape[1:])

    loads = [
        pltpu.make_async_copy(src, dst, load_sem.at[i])
        for i, (src, dst) in enumerate(
            (
                (queries_hbm, queries),
                (keys_hbm, keys),
                (values_hbm, values),
                (outs_hbm, outs),
                (up0.at[:, :, columns(up0, y)], up_own),
                (by_z(down0).at[:, x], down_own),
                (by_z(out0).at[:, x], out_own),
            )
        )
    ]

    def up_y():
        return [remote("up_y", up0.at[:, :, columns(up0, 1 - y)], up1, y_peer)]

    def down_x():
        return [
            remote("down_x", by_z(down0).at[:, 1 - x], down1, x_peer),
            remote("out_x", by_z(out0).at[:, 1 - x], out1, x_peer),
        ]

    def up_x():
        return [remote("up_x", by_z(up1).at[:, 1 - x], up2, x_peer)]

    def down_y():
        return [
            remote("down_y", down1.at[:, :, columns(down1, 1 - y)], down2, y_peer),
            remote("out_y", out1.at[:, :, columns(out1, 1 - y)], out2, y_peer),
        ]

    def over_z(name, src, dst):
        return [
            remote((name, k), src.at[lax.rem(z + k + 1, z_size)], dst.at[k], peer)
            for k, peer in enumerate(z_peers)
        ]

    def up_z():
        return over_z("up_z", up2, up3)

    def down_z():
        return over_z("down_z", down2, down3) + over_z("out_z", out2, out3)

    lasts = (up4, down4, out4)

    def to_y():
        return [remote(("to_y", i), last.at[core, y], last.at[core, y], y_peer) for i, last in enumerate(lasts)]

    def to_core(which):
        at = y if which == 0 else 1 - y
        return [
            remote(("to_core", which, i), last.at[core, at], last.at[core, at], core_peer)
            for i, last in enumerate(lasts)
        ]

    def start(copies):
        for copy in copies:
            copy.start()

    def wait(copies):
        for copy in copies:
            copy.wait()

    start(loads)
    greet([core_peer, y_peer] + row_peers)
    start(up_y())
    start(down_x())

    def up_y_done():
        wait(loads[4:5])
        wait(up_y())

        @pl.loop(0, row_size)
        def _(p):
            up1[p] = up1[p] + up_own[p]

        start(up_x())

    def down_x_done():
        wait(loads[5:])
        wait(down_x())

        @pl.loop(0, z_size)
        def _(p):
            down1[p] = down1[p] + down_own[p]
            out1[p] = out1[p] + out_own[p]

        start(down_y())

    def up_x_done():
        wait(up_x())

        @pl.loop(0, z_size)
        def _(p):
            up2[p] = up2[p] + up1[p * x_size + x]

        start(up_z())

    def down_y_done():
        wait(down_y())

        @pl.loop(0, z_size)
        def _(p):
            down2[p] = down2[p] + down1[p, :, columns(down1, y)]
            out2[p] = out2[p] + out1[p, :, columns(out1, y)]

        start(down_z())

    d_kt[...] = jnp.zeros_like(d_kt)
    d_vt[...] = jnp.zeros_like(d_vt)
    whole = heads // 2

    def unpack(p):
        packed = g_in[p]
        parts = []
        for h in range(whole):
            tile = packed[h * local_rows : (h + 1) * local_rows]
            parts += [tile[:, :HEAD_DIM], tile[:, HEAD_DIM:]]
        if heads % 2:
            tile = packed[whole * local_rows :]
            parts.append(jnp.concatenate([tile[:, :HEAD_DIM], tile[:, HEAD_DIM:]], axis=0))
        rows = pl.ds(pl.multiple_of(p * local_rows, 16), local_rows)
        for h, part in enumerate(parts):
            part = part.astype(jnp.float32)
            result = outs[h, rows, :HEAD_DIM].astype(jnp.float32)
            inner = jnp.sum(part * result, axis=-1, keepdims=True)
            wide = jnp.concatenate([part, jnp.zeros_like(part)], axis=-1)
            grads[h, rows] = set_lanes(wide, HEAD_DIM, split_three(-inner))

    def segment(step, _):
        k, h = step // heads, lax.rem(step, heads)
        there = lax.rem(z + k, z_size)
        rows = pl.ds(pl.multiple_of(there * pair, LANES), pair)

        @pl.when(h == 0)
        def _():
            for other in range(x_size):
                p = there * x_size + other
                unpack(p)

        @pl.when(step == 2 * heads + 2)
        def _():
            up_y_done()

        query, grad = queries[h, rows], grads[h, rows]
        query_t = query[:, :HEAD_DIM].T
        grad_t = grad[:, :HEAD_DIM].T
        d_query = jnp.zeros((pair, LANES), jnp.float32)
        for i in range(total // chunk):
            at = pl.ds(i * chunk, chunk)
            key, value = keys[h, at], values[h, at]
            probs = jnp.exp(lax.dot_general(query, key, NT, preferred_element_type=jnp.float32))
            d_probs = lax.dot_general(grad, value, NT, preferred_element_type=jnp.float32)
            d_scores = (probs * d_probs).astype(jnp.bfloat16)
            d_vt[h, :, at] += jnp.dot(grad_t, probs.astype(jnp.bfloat16), preferred_element_type=jnp.float32)
            d_kt[h, :, at] += jnp.dot(query_t, d_scores, preferred_element_type=jnp.float32)
            d_query += jnp.dot(d_scores, key, preferred_element_type=jnp.float32)
        d_q[h, rows] = (d_query[:, :HEAD_DIM] * HEAD_DIM ** (-0.5)).astype(jnp.bfloat16)
        return 0

    wait(loads[:4])
    lax.fori_loop(0, z_size * heads, segment, 0)
    down_x_done()
    for h in range(heads):
        d_k[h] = d_kt[h].T.astype(jnp.bfloat16)
        d_v[h] = d_vt[h].T.astype(jnp.bfloat16)

    d_qkv[...] = jnp.zeros_like(d_qkv)
    d_emb[...] = jnp.zeros_like(d_emb)
    d_gain[...] = jnp.zeros_like(d_gain)
    d_bias[...] = jnp.zeros_like(d_bias)

    def term_copy(shift):
        p = lax.rem(row + shift, row_size)
        return remote(("term", shift), terms.at[p], terms_in.at[row], (tab, p))

    def project(step, _):
        shift = lax.rem(step + 1, z_size)
        there = lax.rem(z + shift, z_size)
        pieces, embeds = [], []
        for other in range(x_size):
            p = there * x_size + other
            rows = pl.ds(pl.multiple_of(p * local_rows, 16), local_rows)
            key_rows = pl.ds(pl.multiple_of(p * ctx_rows, 16), ctx_rows)
            parts = [d_q[h, rows] for h in range(heads)]
            nothing = jnp.zeros((local_rows - ctx_rows, HEAD_DIM), jnp.bfloat16)
            for ref in (d_k, d_v):
                parts += [jnp.concatenate([ref[h, key_rows], nothing], axis=0) for h in range(heads)]
            pieces.append(jnp.concatenate(parts, axis=1))
            embeds.append(feat[p])
        d_three = jnp.concatenate(pieces, axis=0)
        rows_feat = jnp.concatenate(embeds, axis=0)
        embed = jnp.dot(rows_feat, w_emb[...], preferred_element_type=jnp.float32)
        center = embed - jnp.mean(embed, axis=-1, keepdims=True)
        inverse = lax.rsqrt(jnp.mean(center * center, axis=-1, keepdims=True) + EPS)
        normed = center * inverse
        attn_in = (normed * gain[...] + bias[...]).astype(jnp.bfloat16)
        d_in = lax.dot_general(d_three, w_mine[...], NT, preferred_element_type=jnp.float32)
        d_gain[...] += jnp.sum(d_in * normed, axis=0, keepdims=True)
        d_bias[...] += jnp.sum(d_in, axis=0, keepdims=True)
        scaled = d_in * gain[...]
        inner = (
            scaled
            - jnp.mean(scaled, axis=-1, keepdims=True)
            - normed * jnp.mean(scaled * normed, axis=-1, keepdims=True)
        )
        d_norm = (inverse * inner).astype(jnp.bfloat16)
        term = lax.dot_general(d_norm, w_emb[...], NT, preferred_element_type=jnp.float32).astype(jnp.bfloat16)
        d_emb[...] += jnp.dot(rows_feat.T, d_norm, preferred_element_type=jnp.float32)
        d_qkv[...] += jnp.dot(attn_in.T, d_three, preferred_element_type=jnp.float32)
        for other in range(x_size):
            p = there * x_size + other
            terms[p] = term[other * local_rows : (other + 1) * local_rows]
            ahead = lax.rem(p - row + row_size, row_size)
            for s in range(1, row_size):

                @pl.when(ahead == s)
                def _():
                    term_copy(s).start()

        for at, act in ((1, up_x_done), (2, down_y_done)):

            @pl.when(step == at)
            def _():
                act()

        return 0

    lax.fori_loop(0, z_size, project, 0)

    shard = qkv_own.shape[1]
    for p in range(row_size):
        qkv_own[p] = d_qkv[p * shard : (p + 1) * shard].astype(jnp.bfloat16)
    own_rows = jnp.concatenate([own_feat[t] for t in range(own_feat.shape[0])], axis=0)
    own_d = jnp.concatenate([d_branch[t] for t in range(own_feat.shape[0])], axis=0)
    d_own = d_emb[...] + jnp.dot(own_rows.T, own_d, preferred_element_type=jnp.float32)
    slots = d_own.shape[0]
    spare = lax.broadcasted_iota(jnp.int32, d_own.shape, 0) - (slots - vectors.shape[0])
    d_own = jnp.where(spare == 0, d_gain[...], d_own)
    d_own = jnp.where(spare == 1, d_bias[...], d_own)
    for i in range(2, vectors.shape[0]):
        d_own = jnp.where(spare == i, vectors[i : i + 1], d_own)
    emb_rows = emb_own.shape[1]
    for p in range(row_size):
        emb_own[p] = d_own[p * emb_rows : (p + 1) * emb_rows].astype(jnp.bfloat16)

    def tail_core():
        return [
            remote("qkv_core", qkv_own.at[:, half(shard, 1 - core)], qkv_in0, core_peer),
            remote("emb_core", emb_own.at[:, :, columns(emb_own, 1 - core)], emb_in0, core_peer),
            remote("sums_core", sums, sums_in0, core_peer),
        ]

    def tail_row():
        copies = []
        for k, peer in enumerate(row_peers):
            copies += [
                remote(("qkv_row", k), qkv_in0.at[peer[1]], qkv_in1.at[row], peer),
                remote(("emb_row", k), emb_in0.at[peer[1]], emb_in1.at[row], peer),
                remote(("sums_row", k), sums0, sums_in1.at[row], peer),
            ]
        return copies

    start(tail_core())
    wait(tail_core())
    qkv_in0[...] = qkv_in0[...] + qkv_own[:, half(shard, core)]
    emb_in0[...] = emb_in0[...] + emb_own[:, :, columns(emb_own, core)]
    sums0[...] = sums[...] + sums_in0[...]
    start(tail_row())
    qkv_in1[row] = qkv_in0[row]
    emb_in1[row] = emb_in0[row]
    sums_in1[row] = sums0[...]

    terms_in[row] = terms[row]
    for s in range(1, row_size):
        term_copy(s).wait()
    groups = qkv1.shape[0]
    for t in range(own_feat.shape[0]):
        term = lax.dot_general(d_branch[t], w_emb[...], NT, preferred_element_type=jnp.float32)
        for g in range(groups):
            term = term + terms_in[t * groups + g].astype(jnp.float32)
        slot = lax.broadcasted_iota(jnp.int32, (term.shape[1], 1), 0)
        by_slot = (term.T * jnp.where(slot < counts[t], 1.0, 0.0)).astype(jnp.bfloat16)[: ctx_grad.shape[1]]
        ctx_grad[t] = by_slot[:, :ctx_rows]
        qry_grad[t] = by_slot[:, ctx_rows:]

    wait(up_z())
    wait(down_z())
    for part, taken, last in ((up2, up3, up4), (down2, down3, down4), (out2, out3, out4)):
        whole_sum = part[z].astype(jnp.float32)
        for k in range(z_size - 1):
            whole_sum = whole_sum + taken[k].astype(jnp.float32)
        last[core, y] = whole_sum.astype(jnp.bfloat16)
    start(to_y())
    start(to_core(0))

    wait(tail_row())
    for g in range(groups):
        qkv1[g] = tile_sum(
            [qkv_in1[g + t * groups].astype(jnp.float32) for t in range(row_size // groups)]
        ).astype(jnp.bfloat16)
    emb1[...] = tile_sum([emb_in1[p].astype(jnp.float32) for p in range(row_size)]).astype(jnp.bfloat16)
    sums1[...] = tile_sum([sums_in1[p] for p in range(row_size)])
    tail_y = [
        remote("qkv_y", qkv1, qkv_in2, y_peer),
        remote("emb_y", emb1, emb_in2, y_peer),
        remote("sums_y", sums1, sums_in2, y_peer),
    ]
    start(tail_y)
    wait(to_y())
    start(to_core(1))
    wait(tail_y)
    qkv2[core] = qkv1[...] + qkv_in2[...]
    emb2[:, columns(emb_own, core)] = emb1[...] + emb_in2[...]
    sums_all[...] = sums1[...] + sums_in2[...]
    at_core = columns(emb_own, core)
    tail_last = [
        remote("qkv_last", qkv2.at[core], qkv2.at[core], core_peer),
        remote("emb_last", emb2.at[:, at_core], emb2.at[:, at_core], core_peer),
    ]
    start(tail_last)
    wait(to_core(0))
    wait(to_core(1))
    wait(tail_last)
    emb_row = [remote(("emb_all", k), emb2, emb3.at[row], peer) for k, peer in enumerate(row_peers)]
    start(emb_row)
    emb3[row] = emb2[...]
    for last, result in ((up4, up_all), (down4, down_all), (out4, out_all)):
        rows, wide = last.shape[2:]
        for i in range(2):
            for j in range(2):
                result[i * rows : (i + 1) * rows, j * wide : (j + 1) * wide] = last[i, j].astype(jnp.float32)
    width = heads * HEAD_DIM
    for i in range(2):
        parts = [
            qkv2[i, g][:, n * width : (n + 1) * width].astype(jnp.float32) for n in range(3) for g in range(groups)
        ]
        qkv_all[i * (shard // 2) : (i + 1) * (shard // 2)] = jnp.concatenate(parts, axis=1)
    wait(emb_row)
    for p in range(row_size):
        emb_all[p * emb_rows : (p + 1) * emb_rows] = emb3[p].astype(jnp.float32)


def back(counts, halves, queries, keys, values, outs, g_in, feat, w_emb, w_mine, gain, bias, own_feat, d_branch,
         vectors, sums, slot_count, ctx_rows, groups, chunk, collective_id):
    row_size, local_rows, slots = feat.shape
    heads, total, _ = keys.shape
    all_rows = queries.shape[1]
    dmodel = w_emb.shape[1]
    width = heads * HEAD_DIM
    x_size = 2
    z_size = row_size // x_size
    shapes = [(2 * h.shape[1], h.shape[2]) for h in halves]
    bf16 = lambda *shape: pltpu.VMEM(shape, jnp.bfloat16)
    f32 = lambda *shape: pltpu.VMEM(shape, jnp.float32)
    (ru, wu), (rd, wd), (ro, wo) = shapes
    stage1 = [bf16(row_size, ru // 2, wu // 2), bf16(z_size, rd // 2, wd), bf16(z_size, ro // 2, wo)]
    stage2 = [bf16(z_size, r // 2, w // 2) for r, w in shapes]
    stage3 = [bf16(z_size - 1, r // 2, w // 2) for r, w in shapes]
    stage4 = [bf16(2, 2, r // 2, w // 2) for r, w in shapes]
    by_head = bf16(heads, all_rows, LANES)
    shard, emb_rows = dmodel // row_size, slots // row_size
    inputs = [by_head, bf16(*keys.shape), bf16(*keys.shape), by_head]
    attention = [
        by_head, bf16(heads, all_rows, HEAD_DIM),
        f32(heads, HEAD_DIM, total), f32(heads, HEAD_DIM, total),
        bf16(heads, total, HEAD_DIM), bf16(heads, total, HEAD_DIM),
        bf16(*feat.shape), bf16(*feat.shape),
        f32(dmodel, 3 * width), f32(slots, dmodel), f32(1, dmodel), f32(1, dmodel),
    ]
    half_qkv, half_emb = (row_size, shard // 2, 3 * width), (row_size, emb_rows, dmodel // 2)
    tail = [
        bf16(row_size, shard, 3 * width), bf16(row_size, emb_rows, dmodel),
        bf16(*half_qkv), bf16(*half_emb), f32(*sums.shape), f32(*sums.shape),
        bf16(*half_qkv), bf16(*half_emb), f32(row_size, *sums.shape),
        bf16(groups, shard // 2, 3 * width), bf16(emb_rows, dmodel // 2), f32(*sums.shape),
        bf16(groups, shard // 2, 3 * width), bf16(emb_rows, dmodel // 2), f32(*sums.shape),
        bf16(2, groups, shard // 2, 3 * width), bf16(emb_rows, dmodel), bf16(row_size, emb_rows, dmodel),
    ]
    sends = 6 + 3 * (z_size - 1) + 9 + 8 + 5 * (row_size - 1)
    vmem = pl.BlockSpec(memory_space=pltpu.VMEM)
    anywhere = pl.BlockSpec(memory_space=pl.ANY)
    f32_out = lambda *shape: jax.ShapeDtypeStruct(shape, jnp.float32)
    return pl.pallas_call(
        functools.partial(back_kernel, (row_size, x_size, chunk, ctx_rows, local_rows)),
        out_shape=[
            jax.ShapeDtypeStruct((own_feat.shape[0], slot_count, ctx_rows), jnp.bfloat16),
            jax.ShapeDtypeStruct((own_feat.shape[0], slot_count, local_rows - ctx_rows), jnp.bfloat16),
            f32_out(slots, dmodel),
            f32_out(*sums.shape),
            f32_out(shard, 3 * dmodel),
            f32_out(ro, wo),
            f32_out(ru, wu),
            f32_out(rd, wd),
        ],
        in_specs=[pl.BlockSpec(memory_space=pltpu.SMEM)] + [anywhere] * 7 + [vmem] * 10,
        out_specs=[vmem] * 8,
        scratch_shapes=inputs + stage1 + stage1 + stage2 + stage3 + stage4 + attention + tail + [
            pltpu.SemaphoreType.DMA((7,)),
            pltpu.SemaphoreType.DMA((sends,)),
            pltpu.SemaphoreType.DMA((sends,)),
        ],
        compiler_params=pltpu.CompilerParams(
            collective_id=collective_id, has_side_effects=True, vmem_limit_bytes=62 * 2**20
        ),
        name="back",
    )(counts, *halves, queries, keys, values, outs, g_in, feat, w_emb, w_mine, gain, bias, own_feat, d_branch,
      vectors, sums)


def local_by_heads(
    ctx_feat,
    qry_feat,
    feat_count,
    ctx_count,
    qry_count,
    w_emb,
    ln1_gain,
    ln1_bias,
    w_qkv,
    w_out,
    ln2_gain,
    ln2_bias,
    w_up,
    b_up,
    w_down,
    ctx_cot,
    qry_cot,
):
    table_count, slot_count, ctx_rows = ctx_feat.shape
    qry_rows = qry_feat.shape[2]
    local_rows = ctx_rows + qry_rows
    dmodel = w_out.shape[0]
    head_count = dmodel // HEAD_DIM
    row_size = lax.axis_size("row")
    total_ctx = ctx_rows * row_size
    row_index = lax.axis_index("row")
    groups = row_size // table_count
    heads = head_count // groups
    width = heads * HEAD_DIM

    slot_live = (jnp.arange(slot_count)[None, :] < feat_count[:, None]).astype(jnp.bfloat16)
    features = jnp.concatenate([ctx_feat, qry_feat], axis=2) * slot_live[:, :, None]
    by_row = jnp.pad(jnp.transpose(features, (0, 2, 1)), ((0, 0), (0, 0), (0, LANES - slot_count)))
    w_emb_pad = jnp.pad(w_emb, ((0, LANES - slot_count), (0, 0)))
    packed, back_queries, keys, values, outs, table_feat, w_mine = front(
        ctx_count,
        by_row,
        w_emb_pad,
        ln1_gain[None],
        ln1_bias[None],
        w_qkv,
        total_ctx,
        heads,
        groups,
        math.gcd(total_ctx, 1024),
        0,
    )
    ctx_out, qry_out, g_in, up_half, down_half, out_half, d_branch, vectors, sums = middle(
        ctx_count,
        qry_count,
        by_row,
        w_emb_pad,
        ln2_gain[None],
        ln2_bias[None],
        b_up[None],
        packed,
        w_out,
        w_up,
        w_down,
        ctx_cot,
        qry_cot,
        groups,
        heads,
        math.gcd(w_up.shape[1], 512),
        1,
    )
    ctx_feat_grad, qry_feat_grad, emb_all, sums, qkv_all, out_all, up_all, down_all = back(
        feat_count,
        (up_half, down_half, out_half),
        back_queries,
        keys,
        values,
        outs,
        g_in,
        table_feat,
        w_emb_pad,
        w_mine,
        ln1_gain[None],
        ln1_bias[None],
        by_row,
        d_branch,
        vectors,
        sums,
        slot_count,
        ctx_rows,
        groups,
        math.gcd(total_ctx, 512),
        2,
    )
    grad_w_emb = emb_all[:slot_count]
    vectors = emb_all[LANES - vectors.shape[0] :]

    def own(vector):
        size = vector.size // row_size
        return lax.dynamic_slice_in_dim(vector.reshape(-1), row_index * size, size, 0)

    gain1_all, bias1_all, gain2_all, bias2_all = (own(vectors[i]) for i in range(4))
    upbias_all = own(vectors[4:])
    squares, live_rows = sums[0, :4], sums[0, 4]
    rms = jnp.sqrt(squares / (live_rows * dmodel))
    return (
        ctx_out,
        qry_out,
        ctx_feat_grad,
        qry_feat_grad,
        grad_w_emb,
        gain1_all,
        bias1_all,
        qkv_all,
        out_all,
        gain2_all,
        bias2_all,
        up_all,
        upbias_all,
        down_all,
        rms,
    )


def local(ctx_feat, qry_feat, *rest):
    table_count, slot_count, ctx_rows = ctx_feat.shape
    qry_rows = qry_feat.shape[2]
    head_count = rest[6].shape[0] // HEAD_DIM
    row_size = lax.axis_size("row")
    even = row_size % table_count == 0 and head_count % (row_size // table_count) == 0
    whole = slot_count + 4 + rest[10].shape[1] // rest[6].shape[0] <= LANES and row_size % 2 == 0 and ctx_rows % LANES == 0 and qry_rows % 32 == 0
    inner = local_by_heads if even and whole else local_by_rows
    return inner(ctx_feat, qry_feat, *rest)


def solution(mesh):
    in_specs = (
        P("tab", None, "row"),
        P("tab", None, "row"),
        P("tab"),
        P("tab"),
        P("tab"),
        P(),
        P(),
        P(),
        P(),
        P(),
        P(),
        P(),
        P(),
        P(),
        P(),
        P("tab", "row", None),
        P("tab", "row", None),
    )
    out_specs = (
        P("tab", "row", None),
        P("tab", "row", None),
        P("tab", None, "row"),
        P("tab", None, "row"),
        P(),
        P("row"),
        P("row"),
        P("row", None),
        P("row", None),
        P("row"),
        P("row"),
        P("row", None),
        P("row"),
        P("row", None),
        P(),
    )
    return jax.shard_map(local, mesh=mesh, in_specs=in_specs, out_specs=out_specs, check_vma=False)
```

profile of v0, /device:TPU:8, one launch (start us, length us, event | category | flops | bytes accessed | tf_op | source)
XLA Modules:
  0.0 258.9 jit_solution(6269404375791707299)
XLA Ops:
  0.6 1.0 copy.32
  1.7 0.7 compare_convert_fusion
  2.4 0.8 fusion
  3.2 0.7 pad.8.own_feat
  3.9 1.6 pad.9.w_emb
  5.5 1.3 broadcast_in_dim.20.gain
  6.8 1.3 broadcast_in_dim.21.bias
  8.1 1.3 broadcast_in_dim.23.gain
  9.3 1.3 broadcast_in_dim.24.bias
  10.6 54.9 %front.1 = (bf16[8,480,128]{2,1,0:T(8,128)(2,1)}, bf16[3,2560,128]{2,1,0:T(8,128)(2,1)}, bf16[3,2048,128]{2,1,0:T(8,128)(2,1)}, bf16[3,2048,128]{2,1,0:T(8,128)(...) custom-call(s32[2]{0:T(128)} %ctx_count.1, ...), custom_call_target="tpu_custom_call" | custom-call | tf_op jit(solution)/shard_map/front/pallas_call | solution.py:507
  65.5 47.7 %middle.1 = (bf16[2,256,768]{2,1,0:T(8,128)(2,1)}, bf16[2,64,768]{2,1,0:T(8,128)(2,1)}, bf16[8,480,128]{2,1,0:T(8,128)(2,1)}, bf16[8,48,3072]{2,1,0:T(8,128)(2,1...) custom-call(s32[2]{0:T(128)} %ctx_count.1, ...), custom_call_target="tpu_custom_call" | custom-call | tf_op jit(solution)/shard_map/middle/pallas_call | solution.py:734
  113.2 0.0 copy-start.3
  113.2 128.8 %back.1 = (bf16[2,100,256]{2,1,0:T(8,128)(2,1)}, bf16[2,100,64]{2,1,0:T(8,128)(2,1)}, f32[128,768]{1,0:T(8,128)}, f32[8,128]{1,0:T(8,128)}, f32[96,2304]{1,0:T(8...) custom-call(s32[2]{0:T(128)} %counts.3, bf16[8,48,3072]{2,1,0:T(8,128)(2,1)} %get-tuple-element.42.up0, ...), custom_call_target="tpu_custom_call" | custom-call | tf_op jit(solution)/shard_map/back/pallas_call | solution.py:1193
  242.1 0.0 copy-start.5
  242.1 0.0 copy-start.2
  242.1 1.7 copy.33
  243.8 1.5 copy.34
  245.3 1.7 slice.30
  247.0 0.9 fusion.5
  247.9 0.6 fusion.1
  248.5 0.6 fusion.3
  249.1 0.7 slice.35
  249.8 0.7 dynamic_slice.31
  250.5 1.3 slice.37
  252.4 1.2 sqrt_bitcast_fusion
  253.6 0.0 copy-done.3
  253.6 0.9 copy.41
  254.5 0.7 copy.42
  255.2 0.9 copy.43
  256.1 0.7 copy.44
  256.8 1.0 copy.45
  257.8 1.0 copy.46
  (9 shorter events, 0.0 us)
Async XLA Ops:
  113.2 140.4 %copy-start.3 = (bf16[2,256,768]{2,1,0:T(8,128)(2,1)S(1)}, bf16[2,256,768]{2,1,0:T(8,128)(2,1)}, u32[]{:S(2)}) copy-start(bf16[2,256,768]{2,1,0:T(8,128)(2,1)} %get-tuple-element.101) | copy-start | bytes 2359300
  242.1 12.5 %copy-start.5 = (bf16[2,64,768]{2,1,0:T(8,128)(2,1)S(1)}, bf16[2,64,768]{2,1,0:T(8,128)(2,1)}, u32[]{:S(2)}) copy-start(bf16[2,64,768]{2,1,0:T(8,128)(2,1)} %get-tuple-element.102) | copy-start | bytes 589828
  242.1 13.1 %copy-start.2 = (f32[96,2304]{1,0:T(8,128)S(1)}, f32[96,2304]{1,0:T(8,128)}, u32[]{:S(2)}) copy-start(f32[96,2304]{1,0:T(8,128)} %get-tuple-element.108) | copy-start | bytes 2654212
  247.0 9.1 %copy-start.4 = (f32[96,768]{1,0:T(8,128)S(1)}, f32[96,768]{1,0:T(8,128)}, u32[]{:S(2)}) copy-start(f32[96,768]{1,0:T(8,128)} %get-tuple-element.109) | copy-start | bytes 884740
  253.6 3.2 %copy-start.1 = (f32[96,3072]{1,0:T(8,128)S(1)}, f32[96,3072]{1,0:T(8,128)}, u32[]{:S(2)}) copy-start(f32[96,3072]{1,0:T(8,128)} %get-tuple-element.112) | copy-start | bytes 3538948
  255.2 2.6 %copy-start = (f32[384,768]{1,0:T(8,128)S(1)}, f32[384,768]{1,0:T(8,128)}, u32[]{:S(2)}) copy-start(f32[384,768]{1,0:T(8,128)} %get-tuple-element.114) | copy-start | bytes 3538948
where the time goes:
time: 261 us; the launch traced here: 259 us
  Pallas kernels  231 us (89%)
  local copies, waits for them, and re-layouts  23.3 us (9%)
  other arithmetic  2.74 us (1%)
    pallas_call x1, Pallas kernels, back(): pl.pallas_call(functools.partial(back_kernel, (row_size, x_size, chunk, c...  129 us
    pallas_call x1, Pallas kernels, front(): pl.pallas_call(functools.partial(front_kernel, (row_size, x_size, chunk,...  54.9 us
    pallas_call x1, Pallas kernels, middle(): pl.pallas_call(functools.partial(middle_kernel, (row_size, ctx_rows, loca...  47.7 us
    unnamed x21, local copies, waits for them, and re-layouts  9.49 us

commit v1 on v0

--- a/solution.py
+++ b/solution.py
@@ -318,9 +318,9 @@
 
 
 def front_kernel(
-    dims, counts, own_feat, w_emb, gain, bias, w_qkv,
-    out_in, queries_out, keys_out, values_out, outs_out, feat_out, w_out,
-    feat_in, window, w_lanes, w_mine, queries, keys, values, outs, packed, load_sem, store_sem, send_sem, recv_sem,
+    dims, feat_counts, counts, ctx_feat, qry_feat, w_emb_in, gain_in, bias_in, w_qkv,
+    out_in, queries_out, keys_out, values_out, outs_out, feat_out, w_out, own_feat, w_emb,
+    by_slot, feat_in, window, w_lanes, w_mine, queries, keys, values, outs, packed, load_sem, store_sem, send_sem, recv_sem,
 ):
     row_size, x_size, chunk, ctx_rows, local_rows, heads, groups = dims
     z_size = row_size // x_size
@@ -331,6 +331,7 @@
     tab, row = lax.axis_index("tab"), lax.axis_index("row")
     z = row // x_size
     table, group = row // groups, lax.rem(row, groups)
+    tables = own_feat.shape[0]
     row_peers = [(tab, lax.rem(row + k, row_size)) for k in range(1, row_size)]
     numbers = {}
 
@@ -341,9 +342,14 @@
             device_id=peer, device_id_type=MESH,
         )
 
-    def feat_copy(k):
-        peer = row_peers[k]
-        return remote(("feat", k), own_feat.at[peer[1] // groups], feat_in.at[row], peer)
+    def feat_copy(dt, dg):
+        t, g = lax.rem(table + dt, tables), lax.rem(group + dg, groups)
+        if dt == 0:
+            return remote(("near", dg), own_feat.at[table], feat_in.at[row], (tab, table * groups + g))
+        if dg == 0:
+            return remote(("far", dt), own_feat.at[t], feat_in.at[row], (tab, t * groups + group))
+        came = t * groups + group
+        return remote(("passed", dt, dg), feat_in.at[came], feat_in.at[came], (tab, table * groups + g))
 
     def out_copy(shift):
         p = lax.rem(row + shift, row_size)
@@ -358,9 +364,26 @@
 
     for n in range(3):
         window_copy(n).start()
+    by_slot[...] = jnp.zeros_like(by_slot)
+    slots = ctx_feat.shape[0]
+    slot = lax.broadcasted_iota(jnp.int32, (slots, 1), 0)
+    for t in range(tables):
+        live = jnp.where(slot < feat_counts[t], 1.0, 0.0)
+        by_slot[:slots, :ctx_rows] = ctx_feat[:, t].astype(jnp.float32) * live
+        wide = by_slot[...].T
+        own_feat[t, :ctx_rows] = wide[:ctx_rows].astype(jnp.bfloat16)
+        lane = lax.broadcasted_iota(jnp.int32, qry_feat.shape[1:], 1)
+        narrow = jnp.where(lane < feat_counts[t], qry_feat[t].astype(jnp.float32), 0.0)
+        nothing = jnp.zeros((narrow.shape[0], LANES - slots), jnp.float32)
+        own_feat[t, ctx_rows:] = jnp.concatenate([narrow, nothing], axis=1).astype(jnp.bfloat16)
+    w_emb[...] = jnp.zeros_like(w_emb)
+    w_emb[:slots] = w_emb_in[...]
+    gain, bias = gain_in[...][None], bias_in[...][None]
     greet(row_peers)
-    for k in range(row_size - 1):
-        feat_copy(k).start()
+    for dt in range(1, tables):
+        feat_copy(dt, 0).start()
+    for dg in range(1, groups):
+        feat_copy(0, dg).start()
     feat_in[row] = own_feat[table]
     offset = group * width - first
     for n in range(3):
@@ -378,24 +401,35 @@
     w_store.start()
     count = counts[table]
 
+    near = groups // x_size
+
     def project(step, _):
-        there = lax.rem(z + step, z_size)
+        @pl.when(step == 1)
+        def _():
+            for dt in range(1, tables):
+                feat_copy(tables - dt, 0).wait_recv()
+                for dg in range(1, groups):
+                    feat_copy(dt, dg).start()
+
+        there = lax.rem(z // near + step // near, tables) * near + lax.rem(z + step, near)
         embeds = []
         for other in range(x_size):
             p = there * x_size + other
-            shift = lax.rem(p - row + row_size, row_size)
-            for s in range(1, row_size):
-
-                @pl.when(shift == s)
-                def _():
-                    feat_copy(row_size - s - 1).wait_recv()
+            ahead = lax.rem(p // groups - table + tables, tables)
+            across = lax.rem(group - lax.rem(p, groups) + groups, groups)
+            for dt in range(tables):
+                for dg in range(1, groups):
+
+                    @pl.when((ahead == dt) & (across == dg))
+                    def _():
+                        feat_copy(dt, dg).wait_recv()
 
             embeds.append(feat_in[p])
         rows_feat = jnp.concatenate(embeds, axis=0)
         embed = jnp.dot(rows_feat, w_emb[...], preferred_element_type=jnp.float32)
         center = embed - jnp.mean(embed, axis=-1, keepdims=True)
         inverse = lax.rsqrt(jnp.mean(center * center, axis=-1, keepdims=True) + EPS)
-        attn_in = (center * inverse * gain[...] + bias[...]).astype(jnp.bfloat16)
+        attn_in = (center * inverse * gain + bias).astype(jnp.bfloat16)
         projected = jnp.dot(attn_in, w_lanes[...], preferred_element_type=jnp.float32)
         rows = pl.ds(pl.multiple_of(there * pair, LANES), pair)
         lane = lane_of((pair, LANES))
@@ -478,19 +512,22 @@
     ]
     for store in last:
         store.start()
-    for k in range(row_size - 1):
-        feat_copy(k).wait_send()
+    for dt in range(tables):
+        for dg in range(groups):
+            if dt + dg:
+                feat_copy(dt, dg).wait_send()
     for store in [w_store] + stores + last:
         store.wait()
     for s in range(1, row_size):
         out_copy(s).wait()
 
 
-def front(counts, own_feat, w_emb, gain, bias, w_qkv, total_ctx, heads, groups, chunk, collective_id):
+def front(feat_counts, counts, ctx_feat, qry_feat, w_emb, gain, bias, w_qkv, total_ctx, heads, groups, chunk, collective_id):
     row_size = lax.axis_size("row")
-    _, local_rows, slots = own_feat.shape
+    tables, qry_rows, _ = qry_feat.shape
     dmodel = w_emb.shape[1]
     ctx_rows = total_ctx // row_size
+    local_rows, slots = ctx_rows + qry_rows, LANES
     width = heads * HEAD_DIM
     x_size = 2
     span = -(-(width + (HEAD_DIM if width % LANES else 0)) // LANES) * LANES
@@ -508,11 +545,14 @@
         functools.partial(front_kernel, (row_size, x_size, chunk, ctx_rows, local_rows, heads, groups)),
         out_shape=[
             jax.ShapeDtypeStruct(s, jnp.bfloat16)
-            for s in (block, by_query, by_key, by_key, by_query, feat, (dmodel, 3 * width))
+            for s in (
+                block, by_query, by_key, by_key, by_query, feat, (dmodel, 3 * width),
+                (tables, local_rows, slots), (slots, dmodel),
+            )
         ],
-        in_specs=[pl.BlockSpec(memory_space=pltpu.SMEM)] + [vmem] * 4 + [anywhere],
-        out_specs=[anywhere] * 7,
-        scratch_shapes=[pltpu.VMEM(s, jnp.bfloat16) for s in scratch] + [
+        in_specs=[pl.BlockSpec(memory_space=pltpu.SMEM)] * 2 + [vmem] * 5 + [anywhere],
+        out_specs=[anywhere] * 7 + [vmem] * 2,
+        scratch_shapes=[pltpu.VMEM((slots, ctx_rows), jnp.float32)] + [pltpu.VMEM(s, jnp.bfloat16) for s in scratch] + [
             pltpu.SemaphoreType.DMA((3,)),
             pltpu.SemaphoreType.DMA((7,)),
             pltpu.SemaphoreType.DMA((2 * (row_size - 1),)),
@@ -522,7 +562,7 @@
             collective_id=collective_id, has_side_effects=True, vmem_limit_bytes=60 * 2**20
         ),
         name="front",
-    )(counts, own_feat, w_emb, gain, bias, w_qkv)
+    )(feat_counts, counts, ctx_feat, qry_feat, w_emb, gain, bias, w_qkv)
 
 
 def gelu_parts(values):
@@ -531,7 +571,7 @@
 
 
 def middle_kernel(
-    dims, ctx_count, qry_count, own_feat, w_emb, gain, bias, b_up, out_in, w_out_hbm, w_up_hbm, w_down_hbm, ctx_cot, qry_cot,
+    dims, ctx_count, qry_count, own_feat, w_emb, gain_in, bias_in, b_up, out_in, w_out_hbm, w_up_hbm, w_down_hbm, ctx_cot, qry_cot,
     ctx_out, qry_out, g_in, up_half, down_half, out_half, d_branch_out, vectors, sums,
     w_out, w_up, w_down, attn_in, cot, attn_low, mlp_in, mlp_in_t, mixed, normed, d_mlp_in, act, d_hidden, d_up_bias,
     packed, up, down, out, up_in0, down_in0, out_in0, load_sem, store_sem, send_sem, recv_sem,
@@ -554,6 +594,7 @@
             device_id=peer, device_id_type=MESH,
         )
 
+    gain, bias = gain_in[...][None], bias_in[...][None]
     loads = [
         pltpu.make_async_copy(src, dst, load_sem.at[i])
         for i, (src, dst) in enumerate(
@@ -597,7 +638,7 @@
     center = summed - jnp.mean(summed, axis=-1, keepdims=True)
     inverse = lax.rsqrt(jnp.mean(center * center, axis=-1, keepdims=True) + EPS)
     normed[...] = center * inverse
-    mlp_in[...] = (normed[...] * gain[...] + bias[...]).astype(jnp.bfloat16)
+    mlp_in[...] = (normed[...] * gain + bias).astype(jnp.bfloat16)
     for load in loads[2:]:
         load.wait()
     cot[...] = (cot[...].astype(jnp.float32) * valid).astype(jnp.bfloat16)
@@ -620,7 +661,7 @@
 
     lax.fori_loop(0, tiles, first, 0)
     grad_in = d_mlp_in[...]
-    scaled = grad_in * gain[...]
+    scaled = grad_in * gain
     inner = (
         scaled
         - jnp.mean(scaled, axis=-1, keepdims=True)
@@ -669,11 +710,13 @@
     def second(p, _):
         at = pl.ds(pl.multiple_of(p * per, LANES), per)
         piece = act[:, at]
-        d_mlp_in[...] += jnp.dot(piece, w_down[at], preferred_element_type=jnp.float32)
         down[p] = jnp.dot(piece.T, cot[...], preferred_element_type=jnp.float32).astype(jnp.bfloat16)
         d_up = jnp.dot(mlp_in_t[...], d_hidden[:, at], preferred_element_type=jnp.float32).astype(jnp.bfloat16)
         for q in range(row_size):
             up[q, :, at] = d_up[q * shard : (q + 1) * shard]
+        remote("down", down.at[p, half(down, 1 - core)], down_in0.at[p], core_peer).start()
+        remote("up", up.at[:, half(up, 1 - core), at], up_in0.at[:, :, at], core_peer).start()
+        d_mlp_in[...] += jnp.dot(piece, w_down[at], preferred_element_type=jnp.float32)
         return 0
 
     lax.fori_loop(0, row_size, second, 0)
@@ -681,8 +724,6 @@
         remote("up", up.at[:, half(up, 1 - core)], up_in0, core_peer),
         remote("down", down.at[:, half(down, 1 - core)], down_in0, core_peer),
     ]
-    for copy in copies:
-        copy.start()
     mlp = d_mlp_in[...]
     result = (mixed[...] + mlp) * valid
     square_mlp = jnp.sum(valid * mlp * mlp)
@@ -766,17 +807,36 @@
     return total
 
 
+ROW_AXES = ("x", "near", "far")
+ATTEND_STEPS = ((5, 1, 0), (6, 2, 0), (6, 3, 0), (7, 0, 0), (7, 4, 0),
+                (8, 1, 1), (9, 2, 1), (9, 3, 1), (10, 0, 1), (10, 4, 1), (11, 1, 2))
+PROJECT_STEPS = ((0, 2, 2), (0, 3, 2), (0, 0, 2), (0, 4, 2))
+
+
+def plan_streams(shapes):
+    (up_rows, up_wide), (down_rows, down_wide), (out_rows, out_wide) = shapes
+    cut = up_wide * 7 // 12 // (2 * LANES) * 2 * LANES
+    deep = down_rows * 2 // 3 // 16 * 16
+    return (
+        ("up_y", "up", (0, up_rows), (0, cut), ("y", "x", "near", "far")),
+        ("down_x", "down", (0, deep), (0, down_wide), ("x", "near", "y", "far")),
+        ("up_z", "up", (0, up_rows), (cut, up_wide - cut), ("near", "y", "x", "far")),
+        ("down_z", "down", (deep, down_rows - deep), (0, down_wide), ("near", "y", "x", "far")),
+        ("out_y", "out", (0, out_rows), (0, out_wide), ("y", "x", "near", "far")),
+    )
+
+
 def back_kernel(
-    dims, counts, up0, down0, out0, queries_hbm, keys_hbm, values_hbm, outs_hbm, g_in, feat, w_emb, w_mine, gain, bias,
+    dims, counts, up0, down0, out0, queries_hbm, keys_hbm, values_hbm, outs_hbm, g_in, feat, w_emb, w_mine, gain_in, bias_in,
     own_feat, d_branch, vectors, sums,
-    ctx_grad, qry_grad, emb_all, sums_all, qkv_all, out_all, up_all, down_all,
-    queries, keys, values, outs, up_own, down_own, out_own, up1, down1, out1, up2, down2, out2,
-    up3, down3, out3, up4, down4, out4, grads, d_q, d_kt, d_vt, d_k, d_v, terms, terms_in, d_qkv, d_emb, d_gain, d_bias,
+    ctx_grad, qry_grad, emb_all, own_all, qkv_all, out_all, up_all, down_all,
+    queries, keys, values, outs, grads, d_q, d_kt, d_vt, d_k, d_v, terms, terms_in, d_qkv, d_emb, d_gain, d_bias,
     qkv_own, emb_own, qkv_in0, emb_in0, sums_in0, sums0, qkv_in1, emb_in1, sums_in1,
-    qkv1, emb1, sums1, qkv_in2, emb_in2, sums_in2, qkv2, emb2, emb3,
-    load_sem, send_sem, recv_sem,
+    qkv1, emb1, sums1, qkv_in2, emb_in2, sums_in2, qkv2, emb2, emb3, *rest,
 ):
-    row_size, x_size, chunk, ctx_rows, local_rows = dims
+    row_size, x_size, chunk, ctx_rows, local_rows, plan = dims
+    gain, bias = gain_in[...][None], bias_in[...][None]
+    buffers, (load_sem, send_sem, recv_sem) = rest[:-3], rest[-3:]
     z_size = row_size // x_size
     heads, total, _ = keys.shape
     pair = x_size * local_rows
@@ -785,7 +845,6 @@
     x, z = lax.rem(row, x_size), row // x_size
     core_peer, y_peer, x_peer = (tab ^ 1, row), (tab ^ 2, row), (tab, row ^ 1)
     row_peers = [(tab, lax.rem(row + k, row_size)) for k in range(1, row_size)]
-    z_peers = [(tab, lax.rem(z + k, z_size) * x_size + x) for k in range(1, z_size)]
     numbers = {}
 
     def remote(name, src, dst, peer):
@@ -802,55 +861,66 @@
         wide = ref.shape[-1] // 2
         return pl.ds(pl.multiple_of(which * wide, LANES), wide)
 
-    def by_z(ref):
-        return ref.reshape(z_size, x_size, *ref.shape[1:])
-
+    axes = {"y": (y, y_peer)}
+    for bit, axis in enumerate(ROW_AXES):
+        axes[axis] = (lax.rem(row // 2**bit, 2), (tab, row ^ 2**bit))
+    sources = {"up": up0, "down": down0, "out": out0}
+    streams = []
+    for number, (name, source, rows, cols, order) in enumerate(plan):
+        ref = sources[source].reshape(2, 2, 2, *sources[source].shape[1:])
+        ref = ref.at[:, :, :, pl.ds(*rows), pl.ds(*cols)]
+        dims_left, steps = list(ROW_AXES[::-1]), []
+        shape = [2, 2, 2, rows[1], cols[1]]
+        landing = buffers[6 * number : 6 * number + 6]
+        for k, axis in enumerate(order):
+            mine, (here, peer) = [], axes[axis]
+            if axis == "y":
+                wide = shape[-1] // 2
+                kept, sent = (
+                    (slice(None),) * (len(shape) - 1) + (pl.ds(pl.multiple_of(which * wide, LANES), wide),)
+                    for which in (here, 1 - here)
+                )
+                shape = shape[:-1] + [wide]
+            else:
+                at = dims_left.index(axis)
+                kept, sent = ((slice(None),) * at + (which,) for which in (here, 1 - here))
+                dims_left.pop(at)
+                shape = shape[:at] + shape[at + 1 :]
+            copy = remote((name, axis), ref.at[sent], landing[k], peer)
+            own = pltpu.make_async_copy(ref.at[kept], landing[4], load_sem.at[4 + number]) if k == 0 else None
+            steps.append((copy, own, ref.at[kept] if k else landing[4], landing[k]))
+            ref = landing[k]
+        streams.append((steps, landing[5]))
     loads = [
         pltpu.make_async_copy(src, dst, load_sem.at[i])
         for i, (src, dst) in enumerate(
-            (
-                (queries_hbm, queries),
-                (keys_hbm, keys),
-                (values_hbm, values),
-                (outs_hbm, outs),
-                (up0.at[:, :, columns(up0, y)], up_own),
-                (by_z(down0).at[:, x], down_own),
-                (by_z(out0).at[:, x], out_own),
-            )
+            ((queries_hbm, queries), (keys_hbm, keys), (values_hbm, values), (outs_hbm, outs))
         )
     ]
 
-    def up_y():
-        return [remote("up_y", up0.at[:, :, columns(up0, 1 - y)], up1, y_peer)]
-
-    def down_x():
-        return [
-            remote("down_x", by_z(down0).at[:, 1 - x], down1, x_peer),
-            remote("out_x", by_z(out0).at[:, 1 - x], out1, x_peer),
-        ]
-
-    def up_x():
-        return [remote("up_x", by_z(up1).at[:, 1 - x], up2, x_peer)]
-
-    def down_y():
-        return [
-            remote("down_y", down1.at[:, :, columns(down1, 1 - y)], down2, y_peer),
-            remote("out_y", out1.at[:, :, columns(out1, 1 - y)], out2, y_peer),
-        ]
-
-    def over_z(name, src, dst):
-        return [
-            remote((name, k), src.at[lax.rem(z + k + 1, z_size)], dst.at[k], peer)
-            for k, peer in enumerate(z_peers)
-        ]
-
-    def up_z():
-        return over_z("up_z", up2, up3)
-
-    def down_z():
-        return over_z("down_z", down2, down3) + over_z("out_z", out2, out3)
-
-    lasts = (up4, down4, out4)
+    def advance(number, k):
+        steps, last = streams[number]
+        copy, own, mine, taken = steps[k]
+        copy.wait()
+        if own is not None:
+            own.wait()
+        if k + 1 < len(steps):
+            lead = taken.shape[:-2]
+            size = math.prod(lead)
+
+            @pl.loop(0, size)
+            def _(i):
+                at = []
+                for extent in lead[::-1]:
+                    at.insert(0, lax.rem(i, extent))
+                    i = i // extent
+                taken[tuple(at)] = taken[tuple(at)] + mine[tuple(at)]
+
+            steps[k + 1][0].start()
+        else:
+            last[core, y] = taken[...] + mine[...]
+
+    lasts = [last for _, last in streams]
 
     def to_y():
         return [remote(("to_y", i), last.at[core, y], last.at[core, y], y_peer) for i, last in enumerate(lasts)]
@@ -872,49 +942,9 @@
 
     start(loads)
     greet([core_peer, y_peer] + row_peers)
-    start(up_y())
-    start(down_x())
-
-    def up_y_done():
-        wait(loads[4:5])
-        wait(up_y())
-
-        @pl.loop(0, row_size)
-        def _(p):
-            up1[p] = up1[p] + up_own[p]
-
-        start(up_x())
-
-    def down_x_done():
-        wait(loads[5:])
-        wait(down_x())
-
-        @pl.loop(0, z_size)
-        def _(p):
-            down1[p] = down1[p] + down_own[p]
-            out1[p] = out1[p] + out_own[p]
-
-        start(down_y())
-
-    def up_x_done():
-        wait(up_x())
-
-        @pl.loop(0, z_size)
-        def _(p):
-            up2[p] = up2[p] + up1[p * x_size + x]
-
-        start(up_z())
-
-    def down_y_done():
-        wait(down_y())
-
-        @pl.loop(0, z_size)
-        def _(p):
-            down2[p] = down2[p] + down1[p, :, columns(down1, y)]
-            out2[p] = out2[p] + out1[p, :, columns(out1, y)]
-
-        start(down_z())
-
+    for steps, _ in streams:
+        steps[0][0].start()
+        steps[0][1].start()
     d_kt[...] = jnp.zeros_like(d_kt)
     d_vt[...] = jnp.zeros_like(d_vt)
     whole = heads // 2
@@ -947,9 +977,11 @@
                 p = there * x_size + other
                 unpack(p)
 
-        @pl.when(step == 2 * heads + 2)
-        def _():
-            up_y_done()
+        for at, number, k in ATTEND_STEPS:
+
+            @pl.when(step == at)
+            def _():
+                advance(number, k)
 
         query, grad = queries[h, rows], grads[h, rows]
         query_t = query[:, :HEAD_DIM].T
@@ -967,9 +999,8 @@
         d_q[h, rows] = (d_query[:, :HEAD_DIM] * HEAD_DIM ** (-0.5)).astype(jnp.bfloat16)
         return 0
 
-    wait(loads[:4])
+    wait(loads)
     lax.fori_loop(0, z_size * heads, segment, 0)
-    down_x_done()
     for h in range(heads):
         d_k[h] = d_kt[h].T.astype(jnp.bfloat16)
         d_v[h] = d_vt[h].T.astype(jnp.bfloat16)
@@ -1003,11 +1034,11 @@
         center = embed - jnp.mean(embed, axis=-1, keepdims=True)
         inverse = lax.rsqrt(jnp.mean(center * center, axis=-1, keepdims=True) + EPS)
         normed = center * inverse
-        attn_in = (normed * gain[...] + bias[...]).astype(jnp.bfloat16)
+        attn_in = (normed * gain + bias).astype(jnp.bfloat16)
         d_in = lax.dot_general(d_three, w_mine[...], NT, preferred_element_type=jnp.float32)
         d_gain[...] += jnp.sum(d_in * normed, axis=0, keepdims=True)
         d_bias[...] += jnp.sum(d_in, axis=0, keepdims=True)
-        scaled = d_in * gain[...]
+        scaled = d_in * gain
         inner = (
             scaled
             - jnp.mean(scaled, axis=-1, keepdims=True)
@@ -1027,11 +1058,11 @@
                 def _():
                     term_copy(s).start()
 
-        for at, act in ((1, up_x_done), (2, down_y_done)):
+        for at, number, k in PROJECT_STEPS:
 
             @pl.when(step == at)
             def _():
-                act()
+                advance(number, k)
 
         return 0
 
@@ -1043,8 +1074,8 @@
     own_rows = jnp.concatenate([own_feat[t] for t in range(own_feat.shape[0])], axis=0)
     own_d = jnp.concatenate([d_branch[t] for t in range(own_feat.shape[0])], axis=0)
     d_own = d_emb[...] + jnp.dot(own_rows.T, own_d, preferred_element_type=jnp.float32)
-    slots = d_own.shape[0]
-    spare = lax.broadcasted_iota(jnp.int32, d_own.shape, 0) - (slots - vectors.shape[0])
+    slots_all = d_own.shape[0]
+    spare = lax.broadcasted_iota(jnp.int32, d_own.shape, 0) - (slots_all - vectors.shape[0])
     d_own = jnp.where(spare == 0, d_gain[...], d_own)
     d_own = jnp.where(spare == 1, d_bias[...], d_own)
     for i in range(2, vectors.shape[0]):
@@ -1088,18 +1119,14 @@
         term = lax.dot_general(d_branch[t], w_emb[...], NT, preferred_element_type=jnp.float32)
         for g in range(groups):
             term = term + terms_in[t * groups + g].astype(jnp.float32)
-        slot = lax.broadcasted_iota(jnp.int32, (term.shape[1], 1), 0)
-        by_slot = (term.T * jnp.where(slot < counts[t], 1.0, 0.0)).astype(jnp.bfloat16)[: ctx_grad.shape[1]]
-        ctx_grad[t] = by_slot[:, :ctx_rows]
-        qry_grad[t] = by_slot[:, ctx_rows:]
-
-    wait(up_z())
-    wait(down_z())
-    for part, taken, last in ((up2, up3, up4), (down2, down3, down4), (out2, out3, out4)):
-        whole_sum = part[z].astype(jnp.float32)
-        for k in range(z_size - 1):
-            whole_sum = whole_sum + taken[k].astype(jnp.float32)
-        last[core, y] = whole_sum.astype(jnp.bfloat16)
+        slots = qry_grad.shape[2]
+        lane = lane_of(term.shape)
+        term = jnp.where(lane < counts[t], term, 0.0)
+        ctx_grad[:, t] = term[:ctx_rows].T[:slots].astype(jnp.bfloat16)
+        qry_grad[t] = term[ctx_rows:, :slots].astype(jnp.bfloat16)
+
+    for number in range(len(streams)):
+        advance(number, 3)
     start(to_y())
     start(to_core(0))
 
@@ -1121,7 +1148,7 @@
     wait(tail_y)
     qkv2[core] = qkv1[...] + qkv_in2[...]
     emb2[:, columns(emb_own, core)] = emb1[...] + emb_in2[...]
-    sums_all[...] = sums1[...] + sums_in2[...]
+    sums_all = sums1[...] + sums_in2[...]
     at_core = columns(emb_own, core)
     tail_last = [
         remote("qkv_last", qkv2.at[core], qkv2.at[core], core_peer),
@@ -1134,20 +1161,38 @@
     emb_row = [remote(("emb_all", k), emb2, emb3.at[row], peer) for k, peer in enumerate(row_peers)]
     start(emb_row)
     emb3[row] = emb2[...]
-    for last, result in ((up4, up_all), (down4, down_all), (out4, out_all)):
-        rows, wide = last.shape[2:]
+    results = {"up": up_all, "down": down_all, "out": out_all}
+    for (_, source, rows, cols, _), last in zip(plan, lasts):
+        deep, wide = last.shape[2:]
+        half_rows = sources[source].shape[1]
         for i in range(2):
             for j in range(2):
-                result[i * rows : (i + 1) * rows, j * wide : (j + 1) * wide] = last[i, j].astype(jnp.float32)
+                down_at, across = i * half_rows + rows[0], cols[0] + j * wide
+                results[source][down_at : down_at + deep, across : across + wide] = last[i, j]
     width = heads * HEAD_DIM
     for i in range(2):
         parts = [
-            qkv2[i, g][:, n * width : (n + 1) * width].astype(jnp.float32) for n in range(3) for g in range(groups)
+            qkv2[i, g][:, n * width : (n + 1) * width] for n in range(3) for g in range(groups)
         ]
         qkv_all[i * (shard // 2) : (i + 1) * (shard // 2)] = jnp.concatenate(parts, axis=1)
     wait(emb_row)
-    for p in range(row_size):
-        emb_all[p * emb_rows : (p + 1) * emb_rows] = emb3[p].astype(jnp.float32)
+    slot_count = emb_all.shape[0]
+    whole_emb = jnp.concatenate([emb3[p] for p in range(row_size)], axis=0).astype(jnp.float32)
+    emb_all[...] = whole_emb[:slot_count]
+    vec = whole_emb[slots_all - vectors.shape[0] :]
+    dmodel = vec.shape[1]
+    wide = (vectors.shape[0] - 4) * dmodel // row_size
+    own_vec, own_up = vec[:4, :shard], vec[4:5, :wide]
+    for p in range(1, row_size):
+        at = p * wide
+        own_vec = jnp.where(row == p, vec[:4, p * shard : (p + 1) * shard], own_vec)
+        piece = vec[4 + at // dmodel : 5 + at // dmodel, at % dmodel : at % dmodel + wide]
+        own_up = jnp.where(row == p, piece, own_up)
+    own_all[...] = jnp.zeros_like(own_all)
+    own_all[:4, :shard] = own_vec
+    own_all[4:5] = own_up
+    rms = jnp.sqrt(sums_all / (sums_all[:1, 4:5] * dmodel))
+    own_all[5:6, :LANES] = rms[:1]
 
 
 def back(counts, halves, queries, keys, values, outs, g_in, feat, w_emb, w_mine, gain, bias, own_feat, d_branch,
@@ -1162,11 +1207,16 @@
     shapes = [(2 * h.shape[1], h.shape[2]) for h in halves]
     bf16 = lambda *shape: pltpu.VMEM(shape, jnp.bfloat16)
     f32 = lambda *shape: pltpu.VMEM(shape, jnp.float32)
-    (ru, wu), (rd, wd), (ro, wo) = shapes
-    stage1 = [bf16(row_size, ru // 2, wu // 2), bf16(z_size, rd // 2, wd), bf16(z_size, ro // 2, wo)]
-    stage2 = [bf16(z_size, r // 2, w // 2) for r, w in shapes]
-    stage3 = [bf16(z_size - 1, r // 2, w // 2) for r, w in shapes]
-    stage4 = [bf16(2, 2, r // 2, w // 2) for r, w in shapes]
+    plan = plan_streams([h.shape[1:] for h in halves])
+    landings = []
+    for _, _, rows, cols, order in plan:
+        lead, wide, first = 8, cols[1], None
+        for axis in order:
+            lead, wide = (lead, wide // 2) if axis == "y" else (lead // 2, wide)
+            shape = (2,) * (lead.bit_length() - 1) + (rows[1], wide)
+            first = first or shape
+            landings.append(bf16(*shape))
+        landings += [bf16(*first), bf16(2, 2, rows[1], wide)]
     by_head = bf16(heads, all_rows, LANES)
     shard, emb_rows = dmodel // row_size, slots // row_size
     inputs = [by_head, bf16(*keys.shape), bf16(*keys.shape), by_head]
@@ -1186,26 +1236,27 @@
         bf16(groups, shard // 2, 3 * width), bf16(emb_rows, dmodel // 2), f32(*sums.shape),
         bf16(2, groups, shard // 2, 3 * width), bf16(emb_rows, dmodel), bf16(row_size, emb_rows, dmodel),
     ]
-    sends = 6 + 3 * (z_size - 1) + 9 + 8 + 5 * (row_size - 1)
+    sends = 7 * len(plan) + 8 + 5 * (row_size - 1)
     vmem = pl.BlockSpec(memory_space=pltpu.VMEM)
     anywhere = pl.BlockSpec(memory_space=pl.ANY)
     f32_out = lambda *shape: jax.ShapeDtypeStruct(shape, jnp.float32)
+    bf16_out = lambda *shape: jax.ShapeDtypeStruct(shape, jnp.bfloat16)
     return pl.pallas_call(
-        functools.partial(back_kernel, (row_size, x_size, chunk, ctx_rows, local_rows)),
+        functools.partial(back_kernel, (row_size, x_size, chunk, ctx_rows, local_rows, plan)),
         out_shape=[
-            jax.ShapeDtypeStruct((own_feat.shape[0], slot_count, ctx_rows), jnp.bfloat16),
-            jax.ShapeDtypeStruct((own_feat.shape[0], slot_count, local_rows - ctx_rows), jnp.bfloat16),
-            f32_out(slots, dmodel),
-            f32_out(*sums.shape),
-            f32_out(shard, 3 * dmodel),
-            f32_out(ro, wo),
-            f32_out(ru, wu),
-            f32_out(rd, wd),
+            bf16_out(slot_count, own_feat.shape[0], ctx_rows),
+            bf16_out(own_feat.shape[0], local_rows - ctx_rows, slot_count),
+            f32_out(slot_count, dmodel),
+            f32_out(8, (vectors.shape[0] - 4) * dmodel // row_size),
+            bf16_out(shard, 3 * dmodel),
+            bf16_out(*shapes[2]),
+            bf16_out(*shapes[0]),
+            bf16_out(*shapes[1]),
         ],
         in_specs=[pl.BlockSpec(memory_space=pltpu.SMEM)] + [anywhere] * 7 + [vmem] * 10,
         out_specs=[vmem] * 8,
-        scratch_shapes=inputs + stage1 + stage1 + stage2 + stage3 + stage4 + attention + tail + [
-            pltpu.SemaphoreType.DMA((7,)),
+        scratch_shapes=inputs + attention + tail + landings + [
+            pltpu.SemaphoreType.DMA((4 + len(plan),)),
             pltpu.SemaphoreType.DMA((sends,)),
             pltpu.SemaphoreType.DMA((sends,)),
         ],
@@ -1243,21 +1294,16 @@
     head_count = dmodel // HEAD_DIM
     row_size = lax.axis_size("row")
     total_ctx = ctx_rows * row_size
-    row_index = lax.axis_index("row")
     groups = row_size // table_count
     heads = head_count // groups
-    width = heads * HEAD_DIM
-
-    slot_live = (jnp.arange(slot_count)[None, :] < feat_count[:, None]).astype(jnp.bfloat16)
-    features = jnp.concatenate([ctx_feat, qry_feat], axis=2) * slot_live[:, :, None]
-    by_row = jnp.pad(jnp.transpose(features, (0, 2, 1)), ((0, 0), (0, 0), (0, LANES - slot_count)))
-    w_emb_pad = jnp.pad(w_emb, ((0, LANES - slot_count), (0, 0)))
-    packed, back_queries, keys, values, outs, table_feat, w_mine = front(
+    packed, back_queries, keys, values, outs, table_feat, w_mine, by_row, w_emb_pad = front(
+        feat_count,
         ctx_count,
-        by_row,
-        w_emb_pad,
-        ln1_gain[None],
-        ln1_bias[None],
+        jnp.transpose(ctx_feat, (1, 0, 2)),
+        jnp.transpose(qry_feat, (0, 2, 1)),
+        w_emb,
+        ln1_gain,
+        ln1_bias,
         w_qkv,
         total_ctx,
         heads,
@@ -1270,8 +1316,8 @@
         qry_count,
         by_row,
         w_emb_pad,
-        ln2_gain[None],
-        ln2_bias[None],
+        ln2_gain,
+        ln2_bias,
         b_up[None],
         packed,
         w_out,
@@ -1284,7 +1330,7 @@
         math.gcd(w_up.shape[1], 512),
         1,
     )
-    ctx_feat_grad, qry_feat_grad, emb_all, sums, qkv_all, out_all, up_all, down_all = back(
+    ctx_feat_grad, qry_feat_grad, grad_w_emb, own, qkv_all, out_all, up_all, down_all = back(
         feat_count,
         (up_half, down_half, out_half),
         back_queries,
@@ -1295,8 +1341,8 @@
         table_feat,
         w_emb_pad,
         w_mine,
-        ln1_gain[None],
-        ln1_bias[None],
+        ln1_gain,
+        ln1_bias,
         by_row,
         d_branch,
         vectors,
@@ -1307,17 +1353,11 @@
         math.gcd(total_ctx, 512),
         2,
     )
-    grad_w_emb = emb_all[:slot_count]
-    vectors = emb_all[LANES - vectors.shape[0] :]
-
-    def own(vector):
-        size = vector.size // row_size
-        return lax.dynamic_slice_in_dim(vector.reshape(-1), row_index * size, size, 0)
-
-    gain1_all, bias1_all, gain2_all, bias2_all = (own(vectors[i]) for i in range(4))
-    upbias_all = own(vectors[4:])
-    squares, live_rows = sums[0, :4], sums[0, 4]
-    rms = jnp.sqrt(squares / (live_rows * dmodel))
+    qkv_all, out_all, up_all, down_all = (g.astype(jnp.float32) for g in (qkv_all, out_all, up_all, down_all))
+    ctx_feat_grad = jnp.transpose(ctx_feat_grad, (1, 0, 2))
+    qry_feat_grad = jnp.transpose(qry_feat_grad, (0, 2, 1))
+    gain1_all, bias1_all, gain2_all, bias2_all = (own[i, : dmodel // row_size] for i in range(4))
+    upbias_all, rms = own[4], own[5, :4]
     return (
         ctx_out,
         qry_out,
@@ -1343,7 +1383,7 @@
     head_count = rest[6].shape[0] // HEAD_DIM
     row_size = lax.axis_size("row")
     even = row_size % table_count == 0 and head_count % (row_size // table_count) == 0
-    whole = slot_count + 4 + rest[10].shape[1] // rest[6].shape[0] <= LANES and row_size % 2 == 0 and ctx_rows % LANES == 0 and qry_rows % 32 == 0
+    whole = slot_count + 4 + rest[10].shape[1] // rest[6].shape[0] <= LANES and row_size == 8 and ctx_rows % LANES == 0 and qry_rows % 32 == 0
     inner = local_by_heads if even and whole else local_by_rows
     return inner(ctx_feat, qry_feat, *rest)
 

time: 261 us -> 220 us (0.84)
  Pallas kernels: 231 us -> 204 us
  local copies, waits for them, and re-layouts: 23.3 us -> 7.46 us
  other arithmetic: 2.74 us -> 5.9 us
    pallas_call x1, Pallas kernels: 129 us -> 111 us  [back(): pl.pallas_call(functools.partial(back_kernel, (row_size, x_size, chunk, c...]
    pallas_call x1, Pallas kernels: 54.9 us -> 47.9 us  [front(): pl.pallas_call(functools.partial(front_kernel, (row_size, x_size, chunk,...]
    unnamed x21 -> x19, local copies, waits for them, and re-layouts: 9.49 us -> 3.56 us
    convert_element_type x1 -> x4, other arithmetic: 0.73 us -> 5.9 us  [local_by_heads(): g.astype(jnp.float32)]
    broadcast_in_dim x4 -> x0, local copies, waits for them, and re-layouts: 5.07 us -> none  [the longest x1 1.27 us: local_by_heads(): ln2_gain[None]]
    slice x4 -> x1, local copies, waits for them, and re-layouts: 4.61 us -> 1.35 us  [local_by_heads(): upbias_all, rms = (own[4], own[5, :4])]
where the time goes in v1:
time: 220 us; the launch traced here: 218 us
  Pallas kernels  204 us (93%)
  local copies, waits for them, and re-layouts  7.46 us (3%)
  other arithmetic  5.9 us (3%)
    pallas_call x1, Pallas kernels, back(): pl.pallas_call(functools.partial(back_kernel, (row_size, x_size, chunk, c...  111 us
    pallas_call x1, Pallas kernels, front(): pl.pallas_call(functools.partial(front_kernel, (row_size, x_size, chunk,...  47.9 us
    pallas_call x1, Pallas kernels, middle(): pl.pallas_call(functools.partial(middle_kernel, (row_size, ctx_rows, loca...  45.3 us
    convert_element_type x4, other arithmetic, local_by_heads(): g.astype(jnp.float32)  5.9 us

profile of v1, /device:TPU:8, one launch (start us, length us, event | category | flops | bytes accessed | tf_op | source)
XLA Modules:
  0.0 218.4 jit_solution(15795759181350998584)
XLA Ops:
  0.6 47.9 %front.1 = (bf16[8,480,128]{2,1,0:T(8,128)(2,1)}, bf16[3,2560,128]{2,1,0:T(8,128)(2,1)}, bf16[3,2048,128]{2,1,0:T(8,128)(2,1)}, bf16[3,2048,128]{2,1,0:T(8,128)(...) custom-call(s32[2]{0:T(128)} %counts.3, ...), custom_call_target="tpu_custom_call" | custom-call | tf_op jit(solution)/shard_map/front/pallas_call | solution.py:544
  48.6 45.3 %middle.1 = (bf16[2,256,768]{2,1,0:T(8,128)(2,1)}, bf16[2,64,768]{2,1,0:T(8,128)(2,1)}, bf16[8,480,128]{2,1,0:T(8,128)(2,1)}, bf16[8,48,3072]{2,1,0:T(8,128)(2,1...) custom-call(s32[2]{0:T(128)} %ctx_count.1, ...), custom_call_target="tpu_custom_call" | custom-call | tf_op jit(solution)/shard_map/middle/pallas_call | solution.py:775
  93.9 111.1 %back.1 = (bf16[100,2,256]{2,1,0:T(2,128)(2,1)}, bf16[2,64,100]{2,1,0:T(8,128)(2,1)}, f32[100,768]{1,0:T(8,128)}, f32[8,384]{1,0:T(8,128)}, bf16[96,2304]{1,0:T(...) custom-call(s32[2]{0:T(128)} %counts.3, ...), custom_call_target="tpu_custom_call" | custom-call | tf_op jit(solution)/shard_map/back/pallas_call | solution.py:1244
  205.0 0.0 copy-start.2
  205.0 0.0 copy-start.1
  205.0 1.4 slice_bitcast_fusion.1
  206.4 2.0 convert_element_type.12
  208.4 0.0 copy-start
  208.4 1.7 convert_element_type.13
  210.1 0.0 copy-done.2
  210.1 1.1 convert_element_type.14
  211.2 0.0 copy-start.4
  211.2 0.0 copy-start.5
  211.2 1.3 slice_reduce_fusion
  212.6 0.0 copy-done.1
  212.6 0.0 copy-start.6
  212.6 0.0 copy-start.3
  212.6 1.1 convert_element_type.15
  213.7 1.2 slice_bitcast_fusion
  214.9 0.0 copy-done
  214.9 0.9 copy.37
  215.7 0.0 copy-done.4
  215.7 0.7 copy.38
  216.4 0.0 copy-done.5
  216.4 0.6 copy.39
  217.1 0.0 copy-done.6
  217.1 0.6 copy.40
  217.7 0.0 copy-done.3
  217.7 0.7 copy.41
Async XLA Ops:
  205.0 5.1 %copy-start.2 = (bf16[96,3072]{1,0:T(8,128)(2,1)S(1)}, bf16[96,3072]{1,0:T(8,128)(2,1)}, u32[]{:S(2)}) copy-start(bf16[96,3072]{1,0:T(8,128)(2,1)} %get-tuple-element.65) | copy-start | bytes 1769476
  205.0 7.5 %copy-start.1 = (bf16[384,768]{1,0:T(8,128)(2,1)S(1)}, bf16[384,768]{1,0:T(8,128)(2,1)}, u32[]{:S(2)}) copy-start(bf16[384,768]{1,0:T(8,128)(2,1)} %get-tuple-element.66) | copy-start | bytes 1769476
  208.4 6.5 %copy-start = (bf16[2,256,768]{2,1,0:T(8,128)(2,1)S(1)}, bf16[2,256,768]{2,1,0:T(8,128)(2,1)}, u32[]{:S(2)}) copy-start(bf16[2,256,768]{2,1,0:T(8,128)(2,1)} %get-tuple-element.86) | copy-start | bytes 2359300
  211.2 4.5 %copy-start.4 = (bf16[2,64,768]{2,1,0:T(8,128)(2,1)S(1)}, bf16[2,64,768]{2,1,0:T(8,128)(2,1)}, u32[]{:S(2)}) copy-start(bf16[2,64,768]{2,1,0:T(8,128)(2,1)} %get-tuple-element.87) | copy-start | bytes 589828
  211.2 5.2 %copy-start.5 = (bf16[100,2,256]{2,1,0:T(2,128)(2,1)S(1)}, bf16[100,2,256]{2,1,0:T(2,128)(2,1)}, u32[]{:S(2)}) copy-start(bf16[100,2,256]{2,1,0:T(2,128)(2,1)} %get-tuple-element.59) | copy-start | bytes 307204
  212.6 4.5 %copy-start.6 = (bf16[2,64,100]{2,1,0:T(8,128)(2,1)S(1)}, bf16[2,64,100]{2,1,0:T(8,128)(2,1)}, u32[]{:S(2)}) copy-start(bf16[2,64,100]{2,1,0:T(8,128)(2,1)} %get-tuple-element.60) | copy-start | bytes 76804
  212.6 5.1 %copy-start.3 = (f32[100,768]{1,0:T(8,128)S(1)}, f32[100,768]{1,0:T(8,128)}, u32[]{:S(2)}) copy-start(f32[100,768]{1,0:T(8,128)} %get-tuple-element.90) | copy-start | bytes 921604

commit v2 on v1

--- a/solution.py
+++ b/solution.py
@@ -319,8 +319,8 @@
 
 def front_kernel(
     dims, feat_counts, counts, ctx_feat, qry_feat, w_emb_in, gain_in, bias_in, w_qkv,
-    out_in, queries_out, keys_out, values_out, outs_out, feat_out, w_out, own_feat, w_emb,
-    by_slot, feat_in, window, w_lanes, w_mine, queries, keys, values, outs, packed, load_sem, store_sem, send_sem, recv_sem,
+    out_in, queries_out, keys_out, values_out, outs_out, feat_out, w_out, attn_out, own_feat, w_emb,
+    by_slot, attn_all, feat_in, window, w_lanes, w_mine, queries, keys, values, outs, packed, load_sem, store_sem, send_sem, recv_sem,
 ):
     row_size, x_size, chunk, ctx_rows, local_rows, heads, groups = dims
     z_size = row_size // x_size
@@ -432,6 +432,7 @@
         attn_in = (center * inverse * gain + bias).astype(jnp.bfloat16)
         projected = jnp.dot(attn_in, w_lanes[...], preferred_element_type=jnp.float32)
         rows = pl.ds(pl.multiple_of(there * pair, LANES), pair)
+        attn_all[rows] = attn_in
         lane = lane_of((pair, LANES))
         for h in range(heads):
             query = projected[:, h * LANES : (h + 1) * LANES] * HEAD_DIM ** (-0.5)
@@ -457,7 +458,9 @@
     lax.fori_loop(0, z_size, project, 0)
     stores = [
         pltpu.make_async_copy(src, dst, store_sem.at[i + 1])
-        for i, (src, dst) in enumerate(((keys, keys_out), (values, values_out), (feat_in, feat_out)))
+        for i, (src, dst) in enumerate(
+            ((keys, keys_out), (values, values_out), (feat_in, feat_out), (attn_all, attn_out))
+        )
     ]
     for store in stores:
         store.start()
@@ -506,9 +509,9 @@
 
     lax.fori_loop(0, z_size * heads, segment, 0)
     last = [
-        pltpu.make_async_copy(queries, queries_out, store_sem.at[4]),
-        pltpu.make_async_copy(outs, outs_out, store_sem.at[5]),
-        pltpu.make_async_copy(packed.at[row], out_in.at[row], store_sem.at[6]),
+        pltpu.make_async_copy(queries, queries_out, store_sem.at[5]),
+        pltpu.make_async_copy(outs, outs_out, store_sem.at[6]),
+        pltpu.make_async_copy(packed.at[row], out_in.at[row], store_sem.at[7]),
     ]
     for store in last:
         store.start()
@@ -547,14 +550,18 @@
             jax.ShapeDtypeStruct(s, jnp.bfloat16)
             for s in (
                 block, by_query, by_key, by_key, by_query, feat, (dmodel, 3 * width),
+                (row_size * local_rows, dmodel),
                 (tables, local_rows, slots), (slots, dmodel),
             )
         ],
         in_specs=[pl.BlockSpec(memory_space=pltpu.SMEM)] * 2 + [vmem] * 5 + [anywhere],
-        out_specs=[anywhere] * 7 + [vmem] * 2,
-        scratch_shapes=[pltpu.VMEM((slots, ctx_rows), jnp.float32)] + [pltpu.VMEM(s, jnp.bfloat16) for s in scratch] + [
+        out_specs=[anywhere] * 8 + [vmem] * 2,
+        scratch_shapes=[
+            pltpu.VMEM((slots, ctx_rows), jnp.float32),
+            pltpu.VMEM((row_size * local_rows, dmodel), jnp.bfloat16),
+        ] + [pltpu.VMEM(s, jnp.bfloat16) for s in scratch] + [
             pltpu.SemaphoreType.DMA((3,)),
-            pltpu.SemaphoreType.DMA((7,)),
+            pltpu.SemaphoreType.DMA((8,)),
             pltpu.SemaphoreType.DMA((2 * (row_size - 1),)),
             pltpu.SemaphoreType.DMA((2 * (row_size - 1),)),
         ],
@@ -707,23 +714,66 @@
     d_mlp_in[...] = jnp.zeros_like(d_mlp_in)
     per = hidden_size // row_size
 
+    def span_of(p):
+        return pl.ds(pl.multiple_of(p * per, LANES), per)
+
+    def pieces(p):
+        at = span_of(p)
+        return [
+            pltpu.make_async_remote_copy(
+                src_ref=src, dst_ref=dst, send_sem=send_sem.at[first + p], recv_sem=recv_sem.at[first + p],
+                device_id=core_peer, device_id_type=MESH,
+            )
+            for src, dst, first in (
+                (down.at[p, half(down, 1 - core)], down_in0.at[p], row_size),
+                (up.at[:, half(up, 1 - core), at], up_in0.at[:, :, at], 2 * row_size),
+            )
+        ]
+
+    def stored(p):
+        at = span_of(p)
+        return [
+            pltpu.make_async_copy(down_in0.at[p], down_half.at[p], store_sem.at[2 + p]),
+            pltpu.make_async_copy(up_in0.at[:, :, at], up_half.at[:, :, at], store_sem.at[2 + row_size + p]),
+        ]
+
+    def add_piece(p):
+        at = span_of(p)
+        for copy in pieces(p):
+            copy.wait()
+        down_in0[p] = down_in0[p] + down[p, half(down, core)]
+        for q in range(row_size):
+            up_in0[q, :, at] = up_in0[q, :, at] + up[q, half(up, core), at]
+        for store in stored(p):
+            store.start()
+
     def second(p, _):
-        at = pl.ds(pl.multiple_of(p * per, LANES), per)
+        at = span_of(p)
         piece = act[:, at]
         down[p] = jnp.dot(piece.T, cot[...], preferred_element_type=jnp.float32).astype(jnp.bfloat16)
         d_up = jnp.dot(mlp_in_t[...], d_hidden[:, at], preferred_element_type=jnp.float32).astype(jnp.bfloat16)
         for q in range(row_size):
             up[q, :, at] = d_up[q * shard : (q + 1) * shard]
-        remote("down", down.at[p, half(down, 1 - core)], down_in0.at[p], core_peer).start()
-        remote("up", up.at[:, half(up, 1 - core), at], up_in0.at[:, :, at], core_peer).start()
+        for copy in pieces(p):
+            copy.start()
         d_mlp_in[...] += jnp.dot(piece, w_down[at], preferred_element_type=jnp.float32)
+
+        @pl.when(p > 0)
+        def _():
+            add_piece(p - 1)
+
         return 0
 
     lax.fori_loop(0, row_size, second, 0)
-    copies = [
-        remote("up", up.at[:, half(up, 1 - core)], up_in0, core_peer),
-        remote("down", down.at[:, half(down, 1 - core)], down_in0, core_peer),
-    ]
+    add_piece(row_size - 1)
+    out_copy.wait()
+
+    @pl.loop(0, row_size)
+    def _(p):
+        out_in0[p] = out_in0[p] + out[p, half(out, core)]
+
+    out_store = pltpu.make_async_copy(out_in0, out_half, store_sem.at[1])
+    out_store.start()
     mlp = d_mlp_in[...]
     result = (mixed[...] + mlp) * valid
     square_mlp = jnp.sum(valid * mlp * mlp)
@@ -738,21 +788,11 @@
     for i, part in enumerate(parts):
         total = jnp.where(lane == i, part, total)
     sums[...] = total
-    stores = []
-    for i, (copy, mine, taken, result_hbm) in enumerate(
-        ((out_copy, out, out_in0, out_half), (copies[1], down, down_in0, down_half), (copies[0], up, up_in0, up_half))
-    ):
-        copy.wait()
-
-        @pl.loop(0, row_size)
-        def _(p):
-            taken[p] = taken[p] + mine[p, half(mine, core)]
-
-        store = pltpu.make_async_copy(taken, result_hbm, store_sem.at[i + 1])
-        store.start()
-        stores.append(store)
-    for store in stores + [own_g]:
-        store.wait()
+    for p in range(row_size):
+        for store in stored(p):
+            store.wait()
+    out_store.wait()
+    own_g.wait()
     for copy in g_copies:
         copy.wait()
 
@@ -771,7 +811,7 @@
     anywhere = pl.BlockSpec(memory_space=pl.ANY)
     bf16 = lambda *shape: pltpu.VMEM(shape, jnp.bfloat16)
     f32 = lambda *shape: pltpu.VMEM(shape, jnp.float32)
-    sends = row_size - 1 + 3
+    sends = 3 * row_size
     return pl.pallas_call(
         functools.partial(middle_kernel, (row_size, ctx_rows, local_rows, tables, groups, heads, tile)),
         out_shape=[jax.ShapeDtypeStruct(s, jnp.bfloat16) for s in (ctx_cot.shape, qry_cot.shape, out_in.shape, *halves)]
@@ -789,7 +829,7 @@
             bf16(row_size, shard, hidden_size), bf16(row_size, per, dmodel), bf16(row_size, shard, dmodel),
             *[bf16(*s) for s in halves],
             pltpu.SemaphoreType.DMA((4 + 2 * tables,)),
-            pltpu.SemaphoreType.DMA((4,)),
+            pltpu.SemaphoreType.DMA((2 + 2 * row_size,)),
             pltpu.SemaphoreType.DMA((sends,)),
             pltpu.SemaphoreType.DMA((sends,)),
         ],
@@ -808,9 +848,10 @@
 
 
 ROW_AXES = ("x", "near", "far")
-ATTEND_STEPS = ((5, 1, 0), (6, 2, 0), (6, 3, 0), (7, 0, 0), (7, 4, 0),
-                (8, 1, 1), (9, 2, 1), (9, 3, 1), (10, 0, 1), (10, 4, 1), (11, 1, 2))
-PROJECT_STEPS = ((0, 2, 2), (0, 3, 2), (0, 0, 2), (0, 4, 2))
+ATTEND_STEPS = ((5, 1, 0), (5, 2, 0), (5, 3, 0), (5, 0, 0), (5, 4, 0), (7, 1, 1), (7, 2, 1), (7, 3, 1), (8, 0, 1), (8, 4, 1), (9, 1, 2), (9, 2, 2), (9, 3, 2), (10, 0, 2), (10, 4, 2))
+CHAIN_STEPS = ((9, 0, 1), (11, 0, 2))
+LAST_STEPS = ((0, 0, 3), (0, 1, 1))
+GATHER_STEP = 0
 
 
 def plan_streams(shapes):
@@ -827,16 +868,16 @@
 
 
 def back_kernel(
-    dims, counts, up0, down0, out0, queries_hbm, keys_hbm, values_hbm, outs_hbm, g_in, feat, w_emb, w_mine, gain_in, bias_in,
-    own_feat, d_branch, vectors, sums,
+    dims, counts, up0, down0, out0, queries_hbm, keys_hbm, values_hbm, outs_hbm, attn_hbm, g_hbm, feat_hbm, w_mine_hbm, branch_hbm,
+    w_emb, gain_in, bias_in, own_feat, vectors, sums,
     ctx_grad, qry_grad, emb_all, own_all, qkv_all, out_all, up_all, down_all,
-    queries, keys, values, outs, grads, d_q, d_kt, d_vt, d_k, d_v, terms, terms_in, d_qkv, d_emb, d_gain, d_bias,
-    qkv_own, emb_own, qkv_in0, emb_in0, sums_in0, sums0, qkv_in1, emb_in1, sums_in1,
-    qkv1, emb1, sums1, qkv_in2, emb_in2, sums_in2, qkv2, emb2, emb3, *rest,
+    queries, keys, values, outs, attn_in, g_in, feat, w_mine, d_branch, grads, d_q, d_qt, d_kt, d_vt, d_k, d_v, terms, terms_x, terms_z, terms_far, d_emb, d_gain, d_bias,
+    emb_own, emb_in0, sums_in0, sums0, emb_in1, sums_in1, emb1, sums1, emb_in2, sums_in2, emb2, emb3, *rest,
 ):
     row_size, x_size, chunk, ctx_rows, local_rows, plan = dims
     gain, bias = gain_in[...][None], bias_in[...][None]
     buffers, (load_sem, send_sem, recv_sem) = rest[:-3], rest[-3:]
+    chains, buffers = (buffers[:6], buffers[6:12]), buffers[12:]
     z_size = row_size // x_size
     heads, total, _ = keys.shape
     pair = x_size * local_rows
@@ -845,6 +886,7 @@
     x, z = lax.rem(row, x_size), row // x_size
     core_peer, y_peer, x_peer = (tab ^ 1, row), (tab ^ 2, row), (tab, row ^ 1)
     row_peers = [(tab, lax.rem(row + k, row_size)) for k in range(1, row_size)]
+    cross_peers = [(tab ^ 1, peer[1]) for peer in row_peers]
     numbers = {}
 
     def remote(name, src, dst, peer):
@@ -887,14 +929,17 @@
                 dims_left.pop(at)
                 shape = shape[:at] + shape[at + 1 :]
             copy = remote((name, axis), ref.at[sent], landing[k], peer)
-            own = pltpu.make_async_copy(ref.at[kept], landing[4], load_sem.at[4 + number]) if k == 0 else None
+            own = pltpu.make_async_copy(ref.at[kept], landing[4], load_sem.at[9 + number]) if k == 0 else None
             steps.append((copy, own, ref.at[kept] if k else landing[4], landing[k]))
             ref = landing[k]
         streams.append((steps, landing[5]))
     loads = [
         pltpu.make_async_copy(src, dst, load_sem.at[i])
         for i, (src, dst) in enumerate(
-            ((queries_hbm, queries), (keys_hbm, keys), (values_hbm, values), (outs_hbm, outs))
+            (
+                (g_hbm, g_in), (outs_hbm, outs), (queries_hbm, queries), (keys_hbm, keys), (values_hbm, values),
+                (attn_hbm, attn_in), (feat_hbm, feat), (w_mine_hbm, w_mine), (branch_hbm, d_branch),
+            )
         )
     ]
 
@@ -941,10 +986,80 @@
             copy.wait()
 
     start(loads)
-    greet([core_peer, y_peer] + row_peers)
+    greet([core_peer, y_peer] + row_peers + cross_peers)
     for steps, _ in streams:
         steps[0][0].start()
         steps[0][1].start()
+    chains[1][0][...] = jnp.zeros_like(chains[1][0])
+
+    shard = chains[0][0].shape[1]
+    groups = chains[0][3].shape[0]
+
+    def chain_core(i):
+        pay, taken = chains[i][:2]
+        return [remote(("core", i), pay.at[:, half(shard, 1 - core)], taken, core_peer)]
+
+    def chain_row(i):
+        _, ours, taken = chains[i][:3]
+        return [remote(("row", i, k), ours.at[peer[1]], taken.at[row], peer) for k, peer in enumerate(row_peers)]
+
+    def chain_y(i):
+        return [remote(("y", i), chains[i][3], chains[i][4], y_peer)]
+
+    def chain_last(i):
+        last = chains[i][5]
+        return [remote(("last", i), last.at[core], last.at[core], core_peer)]
+
+    def link(i, k):
+        pay, ours, came, total_own, came_y, last = chains[i]
+        if k == 1:
+            wait(chain_core(i))
+            ours[...] = ours[...] + pay[:, half(shard, core)]
+            start(chain_row(i))
+            came[row] = ours[row]
+        elif k == 2:
+            wait(chain_row(i))
+            for g in range(groups):
+                total_own[g] = tile_sum(
+                    [came[g + t * groups].astype(jnp.float32) for t in range(row_size // groups)]
+                ).astype(jnp.bfloat16)
+            start(chain_y(i))
+        elif k == 3:
+            wait(chain_y(i))
+            last[core] = total_own[...] + came_y[...]
+            start(chain_last(i))
+        else:
+            wait(chain_last(i))
+
+    def finish_head(h):
+        d_k[h] = d_kt[h].T.astype(jnp.bfloat16)
+        d_v[h] = d_vt[h].T.astype(jnp.bfloat16)
+        both = jnp.concatenate([d_kt[h], d_vt[h]], axis=0).astype(jnp.bfloat16)
+        from_keys = tile_sum([
+            jnp.dot(
+                both[:, p * ctx_rows : (p + 1) * ctx_rows],
+                attn_in[p * local_rows : p * local_rows + ctx_rows],
+                preferred_element_type=jnp.float32,
+            )
+            for p in range(row_size)
+        ])
+        from_queries = jnp.dot(d_qt[...], attn_in[...], preferred_element_type=jnp.float32)
+        grad = jnp.concatenate([from_queries, from_keys], axis=0).T.astype(jnp.bfloat16)
+        for one in range(heads):
+            i = one // (heads - 1)
+            pay = chains[i][0]
+            each = HEAD_DIM if i else (heads - 1) * HEAD_DIM
+            first = 0 if i else one * HEAD_DIM
+
+            @pl.when(h == one)
+            def _():
+                for n in range(3):
+                    piece = grad[:, n * HEAD_DIM : (n + 1) * HEAD_DIM]
+                    for p in range(row_size):
+                        pay[p, :, n * each + first : n * each + first + HEAD_DIM] = piece[p * shard : (p + 1) * shard]
+                if one >= heads - 2:
+                    start(chain_core(i))
+
     d_kt[...] = jnp.zeros_like(d_kt)
     d_vt[...] = jnp.zeros_like(d_vt)
     whole = heads // 2
@@ -967,21 +1082,21 @@
             grads[h, rows] = set_lanes(wide, HEAD_DIM, split_three(-inner))
 
     def segment(step, _):
-        k, h = step // heads, lax.rem(step, heads)
-        there = lax.rem(z + k, z_size)
+        h, k = step // z_size, lax.rem(step, z_size)
+        there = k
         rows = pl.ds(pl.multiple_of(there * pair, LANES), pair)
 
-        @pl.when(h == 0)
-        def _():
-            for other in range(x_size):
-                p = there * x_size + other
-                unpack(p)
-
-        for at, number, k in ATTEND_STEPS:
+        for at, i, n in CHAIN_STEPS:
 
             @pl.when(step == at)
             def _():
-                advance(number, k)
+                link(i, n)
+
+        for at, number, n in ATTEND_STEPS:
+
+            @pl.when(step == at)
+            def _():
+                advance(number, n)
 
         query, grad = queries[h, rows], grads[h, rows]
         query_t = query[:, :HEAD_DIM].T
@@ -996,27 +1111,56 @@
             d_vt[h, :, at] += jnp.dot(grad_t, probs.astype(jnp.bfloat16), preferred_element_type=jnp.float32)
             d_kt[h, :, at] += jnp.dot(query_t, d_scores, preferred_element_type=jnp.float32)
             d_query += jnp.dot(d_scores, key, preferred_element_type=jnp.float32)
-        d_q[h, rows] = (d_query[:, :HEAD_DIM] * HEAD_DIM ** (-0.5)).astype(jnp.bfloat16)
+        d_query = (d_query[:, :HEAD_DIM] * HEAD_DIM ** (-0.5)).astype(jnp.bfloat16)
+        d_q[h, rows] = d_query
+        d_qt[:, rows] = d_query.T
+
+        @pl.when(step == z_size - 1)
+        def _():
+            wait(loads[5:])
+
+        @pl.when(k == z_size - 1)
+        def _():
+            finish_head(h)
+
         return 0
 
-    wait(loads)
+    wait(loads[:2])
+    for p in range(row_size):
+        unpack(p)
+    wait(loads[2:5])
     lax.fori_loop(0, z_size * heads, segment, 0)
-    for h in range(heads):
-        d_k[h] = d_kt[h].T.astype(jnp.bfloat16)
-        d_v[h] = d_vt[h].T.astype(jnp.bfloat16)
-
-    d_qkv[...] = jnp.zeros_like(d_qkv)
+
     d_emb[...] = jnp.zeros_like(d_emb)
     d_gain[...] = jnp.zeros_like(d_gain)
     d_bias[...] = jnp.zeros_like(d_bias)
 
-    def term_copy(shift):
-        p = lax.rem(row + shift, row_size)
-        return remote(("term", shift), terms.at[p], terms_in.at[row], (tab, p))
+    near_bit, far_bit = lax.rem(z, 2), z // 2
+    near_peer, far_peer = (tab, row ^ 2), (tab, row ^ 4)
+
+    def term_x(k):
+        return remote(("term_x", k), terms.at[k, 1 - x], terms_x.at[k], x_peer)
+
+    def term_near(k):
+        return remote(("term_near", k), terms.at[k, x], terms_z.at[k], near_peer)
+
+    def term_far():
+        return remote("term_far", terms.at[2, x], terms_far, far_peer)
+
+    def term_sum(k):
+        term_x(k).wait()
+        total = terms[k, x].astype(jnp.float32) + terms_x[k].astype(jnp.float32)
+        if k >= 2:
+            term_near(k - 2).wait()
+            total = total + terms_z[k - 2].astype(jnp.float32)
+        terms[k, x] = total.astype(jnp.bfloat16)
+        if k < 2:
+            term_near(k).start()
+        elif k == 2:
+            term_far().start()
 
     def project(step, _):
-        shift = lax.rem(step + 1, z_size)
-        there = lax.rem(z + shift, z_size)
+        there = lax.rem(far_bit + step + 1, 2) * 2 + lax.rem(near_bit + step // 2 + 1, 2)
         pieces, embeds = [], []
         for other in range(x_size):
             p = there * x_size + other
@@ -1034,7 +1178,6 @@
         center = embed - jnp.mean(embed, axis=-1, keepdims=True)
         inverse = lax.rsqrt(jnp.mean(center * center, axis=-1, keepdims=True) + EPS)
         normed = center * inverse
-        attn_in = (normed * gain + bias).astype(jnp.bfloat16)
         d_in = lax.dot_general(d_three, w_mine[...], NT, preferred_element_type=jnp.float32)
         d_gain[...] += jnp.sum(d_in * normed, axis=0, keepdims=True)
         d_bias[...] += jnp.sum(d_in, axis=0, keepdims=True)
@@ -1047,30 +1190,33 @@
         d_norm = (inverse * inner).astype(jnp.bfloat16)
         term = lax.dot_general(d_norm, w_emb[...], NT, preferred_element_type=jnp.float32).astype(jnp.bfloat16)
         d_emb[...] += jnp.dot(rows_feat.T, d_norm, preferred_element_type=jnp.float32)
-        d_qkv[...] += jnp.dot(attn_in.T, d_three, preferred_element_type=jnp.float32)
         for other in range(x_size):
-            p = there * x_size + other
-            terms[p] = term[other * local_rows : (other + 1) * local_rows]
-            ahead = lax.rem(p - row + row_size, row_size)
-            for s in range(1, row_size):
-
-                @pl.when(ahead == s)
-                def _():
-                    term_copy(s).start()
-
-        for at, number, k in PROJECT_STEPS:
+            terms[step, other] = term[other * local_rows : (other + 1) * local_rows]
+        for k in range(z_size):
+
+            @pl.when(step == k)
+            def _():
+                term_x(k).start()
+                if k:
+                    term_sum(k - 1)
+
+        @pl.when(step == GATHER_STEP)
+        def _():
+            for number in range(len(streams)):
+                advance(number, 3)
+            start(to_y())
+            start(to_core(0))
+
+        for at, i, n in LAST_STEPS:
 
             @pl.when(step == at)
             def _():
-                advance(number, k)
+                link(i, n)
 
         return 0
 
     lax.fori_loop(0, z_size, project, 0)
 
-    shard = qkv_own.shape[1]
-    for p in range(row_size):
-        qkv_own[p] = d_qkv[p * shard : (p + 1) * shard].astype(jnp.bfloat16)
     own_rows = jnp.concatenate([own_feat[t] for t in range(own_feat.shape[0])], axis=0)
     own_d = jnp.concatenate([d_branch[t] for t in range(own_feat.shape[0])], axis=0)
     d_own = d_emb[...] + jnp.dot(own_rows.T, own_d, preferred_element_type=jnp.float32)
@@ -1086,7 +1232,6 @@
 
     def tail_core():
         return [
-            remote("qkv_core", qkv_own.at[:, half(shard, 1 - core)], qkv_in0, core_peer),
             remote("emb_core", emb_own.at[:, :, columns(emb_own, 1 - core)], emb_in0, core_peer),
             remote("sums_core", sums, sums_in0, core_peer),
         ]
@@ -1095,72 +1240,69 @@
         copies = []
         for k, peer in enumerate(row_peers):
             copies += [
-                remote(("qkv_row", k), qkv_in0.at[peer[1]], qkv_in1.at[row], peer),
                 remote(("emb_row", k), emb_in0.at[peer[1]], emb_in1.at[row], peer),
                 remote(("sums_row", k), sums0, sums_in1.at[row], peer),
             ]
         return copies
 
+    def tail_y():
+        return [remote("emb_y", emb1, emb_in2, y_peer), remote("sums_y", sums1, sums_in2, y_peer)]
+
+    at_core = columns(emb_own, core)
+
+    def tail_all():
+        peers = row_peers + [core_peer] + cross_peers
+        return [
+            remote(("emb_all", k), emb2, emb3.at[row, :, at_core], peer) for k, peer in enumerate(peers)
+        ]
+
     start(tail_core())
+    link(1, 2)
     wait(tail_core())
-    qkv_in0[...] = qkv_in0[...] + qkv_own[:, half(shard, core)]
-    emb_in0[...] = emb_in0[...] + emb_own[:, :, columns(emb_own, core)]
+    emb_in0[...] = emb_in0[...] + emb_own[:, :, at_core]
     sums0[...] = sums[...] + sums_in0[...]
     start(tail_row())
-    qkv_in1[row] = qkv_in0[row]
     emb_in1[row] = emb_in0[row]
     sums_in1[row] = sums0[...]
-
-    terms_in[row] = terms[row]
-    for s in range(1, row_size):
-        term_copy(s).wait()
-    groups = qkv1.shape[0]
+    wait(to_y())
+    start(to_core(1))
+
+    term_sum(z_size - 1)
+    term_far().wait()
     for t in range(own_feat.shape[0]):
         term = lax.dot_general(d_branch[t], w_emb[...], NT, preferred_element_type=jnp.float32)
-        for g in range(groups):
-            term = term + terms_in[t * groups + g].astype(jnp.float32)
+        from_heads = jnp.where(far_bit == t, terms[z_size - 1, x].astype(jnp.float32), terms_far[...].astype(jnp.float32))
+        term = term + from_heads
         slots = qry_grad.shape[2]
         lane = lane_of(term.shape)
         term = jnp.where(lane < counts[t], term, 0.0)
         ctx_grad[:, t] = term[:ctx_rows].T[:slots].astype(jnp.bfloat16)
         qry_grad[t] = term[ctx_rows:, :slots].astype(jnp.bfloat16)
 
-    for number in range(len(streams)):
-        advance(number, 3)
-    start(to_y())
-    start(to_core(0))
-
     wait(tail_row())
-    for g in range(groups):
-        qkv1[g] = tile_sum(
-            [qkv_in1[g + t * groups].astype(jnp.float32) for t in range(row_size // groups)]
-        ).astype(jnp.bfloat16)
     emb1[...] = tile_sum([emb_in1[p].astype(jnp.float32) for p in range(row_size)]).astype(jnp.bfloat16)
     sums1[...] = tile_sum([sums_in1[p] for p in range(row_size)])
-    tail_y = [
-        remote("qkv_y", qkv1, qkv_in2, y_peer),
-        remote("emb_y", emb1, emb_in2, y_peer),
-        remote("sums_y", sums1, sums_in2, y_peer),
-    ]
-    start(tail_y)
-    wait(to_y())
-    start(to_core(1))
-    wait(tail_y)
-    qkv2[core] = qkv1[...] + qkv_in2[...]
-    emb2[:, columns(emb_own, core)] = emb1[...] + emb_in2[...]
+    start(tail_y())
+    link(1, 3)
+    wait(tail_y())
+    emb2[...] = emb1[...] + emb_in2[...]
     sums_all = sums1[...] + sums_in2[...]
-    at_core = columns(emb_own, core)
-    tail_last = [
-        remote("qkv_last", qkv2.at[core], qkv2.at[core], core_peer),
-        remote("emb_last", emb2.at[:, at_core], emb2.at[:, at_core], core_peer),
-    ]
-    start(tail_last)
+    start(tail_all())
+    emb3[row, :, at_core] = emb2[...]
+    link(0, 4)
+    link(1, 4)
+    for i in range(2):
+        parts = []
+        for n in range(3):
+            for g in range(groups):
+                for h in range(heads):
+                    which = h // (heads - 1)
+                    each = HEAD_DIM if which else (heads - 1) * HEAD_DIM
+                    first = n * each + (0 if which else h * HEAD_DIM)
+                    parts.append(chains[which][5][i, g][:, first : first + HEAD_DIM])
+        qkv_all[i * (shard // 2) : (i + 1) * (shard // 2)] = jnp.concatenate(parts, axis=1)
     wait(to_core(0))
     wait(to_core(1))
-    wait(tail_last)
-    emb_row = [remote(("emb_all", k), emb2, emb3.at[row], peer) for k, peer in enumerate(row_peers)]
-    start(emb_row)
-    emb3[row] = emb2[...]
     results = {"up": up_all, "down": down_all, "out": out_all}
     for (_, source, rows, cols, _), last in zip(plan, lasts):
         deep, wide = last.shape[2:]
@@ -1169,13 +1311,7 @@
             for j in range(2):
                 down_at, across = i * half_rows + rows[0], cols[0] + j * wide
                 results[source][down_at : down_at + deep, across : across + wide] = last[i, j]
-    width = heads * HEAD_DIM
-    for i in range(2):
-        parts = [
-            qkv2[i, g][:, n * width : (n + 1) * width] for n in range(3) for g in range(groups)
-        ]
-        qkv_all[i * (shard // 2) : (i + 1) * (shard // 2)] = jnp.concatenate(parts, axis=1)
-    wait(emb_row)
+    wait(tail_all())
     slot_count = emb_all.shape[0]
     whole_emb = jnp.concatenate([emb3[p] for p in range(row_size)], axis=0).astype(jnp.float32)
     emb_all[...] = whole_emb[:slot_count]
@@ -1195,7 +1331,7 @@
     own_all[5:6, :LANES] = rms[:1]
 
 
-def back(counts, halves, queries, keys, values, outs, g_in, feat, w_emb, w_mine, gain, bias, own_feat, d_branch,
+def back(counts, halves, queries, keys, values, outs, attn_in, g_in, feat, w_emb, w_mine, gain, bias, own_feat, d_branch,
          vectors, sums, slot_count, ctx_rows, groups, chunk, collective_id):
     row_size, local_rows, slots = feat.shape
     heads, total, _ = keys.shape
@@ -1220,23 +1356,26 @@
     by_head = bf16(heads, all_rows, LANES)
     shard, emb_rows = dmodel // row_size, slots // row_size
     inputs = [by_head, bf16(*keys.shape), bf16(*keys.shape), by_head]
+    inputs += [bf16(*a.shape) for a in (attn_in, g_in, feat, w_mine, d_branch)]
     attention = [
-        by_head, bf16(heads, all_rows, HEAD_DIM),
+        by_head, bf16(heads, all_rows, HEAD_DIM), bf16(HEAD_DIM, all_rows),
         f32(heads, HEAD_DIM, total), f32(heads, HEAD_DIM, total),
         bf16(heads, total, HEAD_DIM), bf16(heads, total, HEAD_DIM),
-        bf16(*feat.shape), bf16(*feat.shape),
-        f32(dmodel, 3 * width), f32(slots, dmodel), f32(1, dmodel), f32(1, dmodel),
+        bf16(z_size, x_size, local_rows, slots), bf16(z_size, local_rows, slots), bf16(2, local_rows, slots),
+        bf16(local_rows, slots),
+        f32(slots, dmodel), f32(1, dmodel), f32(1, dmodel),
     ]
-    half_qkv, half_emb = (row_size, shard // 2, 3 * width), (row_size, emb_rows, dmodel // 2)
+    half_emb = (row_size, emb_rows, dmodel // 2)
     tail = [
-        bf16(row_size, shard, 3 * width), bf16(row_size, emb_rows, dmodel),
-        bf16(*half_qkv), bf16(*half_emb), f32(*sums.shape), f32(*sums.shape),
-        bf16(*half_qkv), bf16(*half_emb), f32(row_size, *sums.shape),
-        bf16(groups, shard // 2, 3 * width), bf16(emb_rows, dmodel // 2), f32(*sums.shape),
-        bf16(groups, shard // 2, 3 * width), bf16(emb_rows, dmodel // 2), f32(*sums.shape),
-        bf16(2, groups, shard // 2, 3 * width), bf16(emb_rows, dmodel), bf16(row_size, emb_rows, dmodel),
+        bf16(row_size, emb_rows, dmodel), bf16(*half_emb), f32(*sums.shape), f32(*sums.shape),
+        bf16(*half_emb), f32(row_size, *sums.shape), bf16(emb_rows, dmodel // 2), f32(*sums.shape),
+        bf16(emb_rows, dmodel // 2), f32(*sums.shape), bf16(emb_rows, dmodel // 2), bf16(row_size, emb_rows, dmodel),
     ]
-    sends = 7 * len(plan) + 8 + 5 * (row_size - 1)
+    for each in (heads - 1, 1):
+        wide = -(-3 * each * HEAD_DIM // LANES) * LANES
+        mine, ours = (row_size, shard // 2, wide), (groups, shard // 2, wide)
+        tail += [bf16(row_size, shard, wide), bf16(*mine), bf16(*mine), bf16(*ours), bf16(*ours), bf16(2, *ours)]
+    sends = 7 * len(plan) + 18 + 6 * (row_size - 1)
     vmem = pl.BlockSpec(memory_space=pltpu.VMEM)
     anywhere = pl.BlockSpec(memory_space=pl.ANY)
     f32_out = lambda *shape: jax.ShapeDtypeStruct(shape, jnp.float32)
@@ -1253,10 +1392,10 @@
             bf16_out(*shapes[0]),
             bf16_out(*shapes[1]),
         ],
-        in_specs=[pl.BlockSpec(memory_space=pltpu.SMEM)] + [anywhere] * 7 + [vmem] * 10,
+        in_specs=[pl.BlockSpec(memory_space=pltpu.SMEM)] + [anywhere] * 12 + [vmem] * 6,
         out_specs=[vmem] * 8,
         scratch_shapes=inputs + attention + tail + landings + [
-            pltpu.SemaphoreType.DMA((4 + len(plan),)),
+            pltpu.SemaphoreType.DMA((9 + len(plan),)),
             pltpu.SemaphoreType.DMA((sends,)),
             pltpu.SemaphoreType.DMA((sends,)),
         ],
@@ -1264,8 +1403,48 @@
             collective_id=collective_id, has_side_effects=True, vmem_limit_bytes=62 * 2**20
         ),
         name="back",
-    )(counts, *halves, queries, keys, values, outs, g_in, feat, w_emb, w_mine, gain, bias, own_feat, d_branch,
+    )(counts, *halves, queries, keys, values, outs, attn_in, g_in, feat, w_mine, d_branch, w_emb, gain, bias, own_feat,
       vectors, sums)
+
+
+def finish(own, lengths, kept, widened):
+    sources = [*kept, *widened]
+    count = len(sources)
+
+    def kernel(own_ref, *refs):
+        vectors, refs = refs[count : count + len(lengths)], refs[:count] + refs[count + len(lengths) :]
+        ins, outs, held = refs[:count], refs[count : 2 * count], refs[2 * count : 3 * count]
+        wide, (in_sem, out_sem) = refs[3 * count : -2], refs[-2:]
+        loads = [pltpu.make_async_copy(ins[i], held[i], in_sem.at[i]) for i in range(count)]
+        for load in loads:
+            load.start()
+        for i, size in enumerate(lengths):
+            vectors[i][...] = own_ref[i, :size]
+        stores = []
+        for i, load in enumerate(loads):
+            load.wait()
+            ready = held[i]
+            if i >= len(kept):
+                ready = wide[i - len(kept)]
+                ready[...] = held[i][...].astype(jnp.float32)
+            stores.append(pltpu.make_async_copy(ready, outs[i], out_sem.at[i]))
+            stores[-1].start()
+        for store in stores:
+            store.wait()
+
+    return pl.pallas_call(
+        kernel,
+        out_shape=[jax.ShapeDtypeStruct((size,), jnp.float32) for size in lengths]
+        + [jax.ShapeDtypeStruct(a.shape, a.dtype) for a in kept]
+        + [jax.ShapeDtypeStruct(a.shape, jnp.float32) for a in widened],
+        in_specs=[pl.BlockSpec(memory_space=pltpu.VMEM)] + [pl.BlockSpec(memory_space=pl.ANY)] * count,
+        out_specs=[pl.BlockSpec(memory_space=pltpu.VMEM)] * len(lengths) + [pl.BlockSpec(memory_space=pl.ANY)] * count,
+        scratch_shapes=[pltpu.VMEM(a.shape, a.dtype) for a in sources]
+        + [pltpu.VMEM(a.shape, jnp.float32) for a in widened]
+        + [pltpu.SemaphoreType.DMA((count,))] * 2,
+        compiler_params=pltpu.CompilerParams(vmem_limit_bytes=62 * 2**20),
+        name="finish",
+    )(own, *sources)
 
 
 def local_by_heads(
@@ -1296,7 +1475,7 @@
     total_ctx = ctx_rows * row_size
     groups = row_size // table_count
     heads = head_count // groups
-    packed, back_queries, keys, values, outs, table_feat, w_mine, by_row, w_emb_pad = front(
+    packed, back_queries, keys, values, outs, table_feat, w_mine, attn_in, by_row, w_emb_pad = front(
         feat_count,
         ctx_count,
         jnp.transpose(ctx_feat, (1, 0, 2)),
@@ -1337,6 +1516,7 @@
         keys,
         values,
         outs,
+        attn_in,
         g_in,
         table_feat,
         w_emb_pad,
@@ -1353,11 +1533,16 @@
         math.gcd(total_ctx, 512),
         2,
     )
-    qkv_all, out_all, up_all, down_all = (g.astype(jnp.float32) for g in (qkv_all, out_all, up_all, down_all))
+    shard = dmodel // row_size
+    (
+        gain1_all, bias1_all, gain2_all, bias2_all, upbias_all, rms,
+        ctx_out, qry_out, ctx_feat_grad, qry_feat_grad, grad_w_emb, up_all, down_all, qkv_all, out_all,
+    ) = finish(
+        own, (shard,) * 4 + (w_up.shape[1] // row_size, 4),
+        (ctx_out, qry_out, ctx_feat_grad, qry_feat_grad, grad_w_emb), (up_all, down_all, qkv_all, out_all)
+    )
     ctx_feat_grad = jnp.transpose(ctx_feat_grad, (1, 0, 2))
     qry_feat_grad = jnp.transpose(qry_feat_grad, (0, 2, 1))
-    gain1_all, bias1_all, gain2_all, bias2_all = (own[i, : dmodel // row_size] for i in range(4))
-    upbias_all, rms = own[4], own[5, :4]
     return (
         ctx_out,
         qry_out,
@@ -1382,8 +1567,8 @@
     qry_rows = qry_feat.shape[2]
     head_count = rest[6].shape[0] // HEAD_DIM
     row_size = lax.axis_size("row")
-    even = row_size % table_count == 0 and head_count % (row_size // table_count) == 0
-    whole = slot_count + 4 + rest[10].shape[1] // rest[6].shape[0] <= LANES and row_size == 8 and ctx_rows % LANES == 0 and qry_rows % 32 == 0
+    even = row_size % table_count == 0 and head_count % (row_size // table_count) == 0 and head_count // (row_size // table_count) > 1
+    whole = slot_count + 4 + rest[10].shape[1] // rest[6].shape[0] <= LANES and row_size == 8 and table_count == 2 and ctx_rows % LANES == 0 and qry_rows % 32 == 0
     inner = local_by_heads if even and whole else local_by_rows
     return inner(ctx_feat, qry_feat, *rest)
 

time: 220 us -> 195 us (0.89)
  Pallas kernels: 204 us -> 192 us
  local copies, waits for them, and re-layouts: 7.46 us -> 0 us
  other arithmetic: 5.9 us -> 0 us
    pallas_call x1, Pallas kernels: 111 us -> 94.1 us  [back(): pl.pallas_call(functools.partial(back_kernel, (row_size, x_size, chunk, c...]
    convert_element_type x4 -> x0, other arithmetic: 5.9 us -> none  [local_by_heads(): g.astype(jnp.float32)]
    pallas_call x0 -> x1, Pallas kernels: none -> 4.85 us  [finish(): pl.pallas_call(kernel, out_shape=[jax.ShapeDtypeStruct((size,), jnp.float...]
    unnamed x19 -> x0, local copies, waits for them, and re-layouts: 3.56 us -> none
    squeeze x2 -> x0, local copies, waits for them, and re-layouts: 2.55 us -> none  [the longest x1 1.36 us: local_by_heads(): own[i, :dmodel // row_size]]
where the time goes in v2:
time: 195 us; the launch traced here: 193 us
  Pallas kernels  192 us (98%)
    pallas_call x1, Pallas kernels, back(): pl.pallas_call(functools.partial(back_kernel, (row_size, x_size, chunk, c...  94.1 us
    pallas_call x1, Pallas kernels, front(): pl.pallas_call(functools.partial(front_kernel, (row_size, x_size, chunk,...  48 us
    pallas_call x1, Pallas kernels, middle(): pl.pallas_call(functools.partial(middle_kernel, (row_size, ctx_rows, loca...  44.9 us
    pallas_call x1, Pallas kernels, finish(): pl.pallas_call(kernel, out_shape=[jax.ShapeDtypeStruct((size,), jnp.float...  4.85 us

profile of v2, /device:TPU:8, one launch (start us, length us, event | category | flops | bytes accessed | tf_op | source)
XLA Modules:
  0.0 192.6 jit_solution(17217111847291414522)
XLA Ops:
  0.6 48.0 %front.1 = (bf16[8,480,128]{2,1,0:T(8,128)(2,1)}, bf16[3,2560,128]{2,1,0:T(8,128)(2,1)}, bf16[3,2048,128]{2,1,0:T(8,128)(2,1)}, bf16[3,2048,128]{2,1,0:T(8,128)(...) custom-call(s32[2]{0:T(128)} %counts.3, ...), custom_call_target="tpu_custom_call" | custom-call | tf_op jit(solution)/shard_map/front/pallas_call | solution.py:547
  48.6 44.9 %middle.1 = (bf16[2,256,768]{2,1,0:T(8,128)(2,1)}, bf16[2,64,768]{2,1,0:T(8,128)(2,1)}, bf16[8,480,128]{2,1,0:T(8,128)(2,1)}, bf16[8,48,3072]{2,1,0:T(8,128)(2,1...) custom-call(s32[2]{0:T(128)} %ctx_count.1, ...), custom_call_target="tpu_custom_call" | custom-call | tf_op jit(solution)/shard_map/middle/pallas_call | solution.py:815
  93.5 94.1 %back.1 = (bf16[100,2,256]{2,1,0:T(2,128)(2,1)}, bf16[2,64,100]{2,1,0:T(8,128)(2,1)}, f32[100,768]{1,0:T(8,128)}, f32[8,384]{1,0:T(8,128)}, bf16[96,2304]{1,0:T(...) custom-call(s32[2]{0:T(128)} %counts.3, ...), custom_call_target="tpu_custom_call" | custom-call | tf_op jit(solution)/shard_map/back/pallas_call | solution.py:1383
  187.6 4.8 %finish.1 = (f32[96]{0:T(128)}, f32[96]{0:T(128)}, f32[96]{0:T(128)}, f32[96]{0:T(128)}, f32[384]{0:T(512)}, /*index=5*/f32[4]{0:T(128)}, bf16[2,256,768]{2,1,0:...) custom-call(f32[8,384]{1,0:T(8,128)} %get-tuple-element.74.own_ref, ...), custom_call_target="tpu_custom_call" | custom-call | tf_op jit(solution)/shard_map/finish/pallas_call | solution.py:1435

commit v3 on v2

--- a/solution.py
+++ b/solution.py
@@ -580,7 +580,7 @@
 def middle_kernel(
     dims, ctx_count, qry_count, own_feat, w_emb, gain_in, bias_in, b_up, out_in, w_out_hbm, w_up_hbm, w_down_hbm, ctx_cot, qry_cot,
     ctx_out, qry_out, g_in, up_half, down_half, out_half, d_branch_out, vectors, sums,
-    w_out, w_up, w_down, attn_in, cot, attn_low, mlp_in, mlp_in_t, mixed, normed, d_mlp_in, act, d_hidden, d_up_bias,
+    w_out, w_up, w_down, attn_in, cot, attn_low, mlp_in, mlp_in_t, mixed, normed, inverses, d_mlp_in, act, d_hidden, d_up_bias,
     packed, up, down, out, up_in0, down_in0, out_in0, load_sem, store_sem, send_sem, recv_sem,
 ):
     row_size, ctx_rows, local_rows, tables, groups, heads, tile = dims
@@ -645,6 +645,7 @@
     center = summed - jnp.mean(summed, axis=-1, keepdims=True)
     inverse = lax.rsqrt(jnp.mean(center * center, axis=-1, keepdims=True) + EPS)
     normed[...] = center * inverse
+    inverses[...] = inverse
     mlp_in[...] = (normed[...] * gain + bias).astype(jnp.bfloat16)
     for load in loads[2:]:
         load.wait()
@@ -654,39 +655,42 @@
     def columns(i):
         return pl.ds(pl.multiple_of(i * tile, LANES), tile)
 
-    def first(i, _):
-        at = columns(i)
-        hidden = jnp.dot(mlp_in[...], w_up[:, at], preferred_element_type=jnp.float32) + b_up[:, at]
-        d_act = lax.dot_general(cot[...], w_down[at], NT, preferred_element_type=jnp.float32)
-        below, slope = gelu_parts(hidden)
-        act[:, at] = (hidden * below).astype(jnp.bfloat16)
-        grad = (d_act * (below + slope)).astype(jnp.bfloat16)
-        d_hidden[:, at] = grad
-        d_up_bias[:, at] = jnp.sum(grad.astype(jnp.float32), axis=0, keepdims=True)
-        d_mlp_in[...] += lax.dot_general(grad, w_up[:, at], NT, preferred_element_type=jnp.float32)
-        return 0
-
-    lax.fori_loop(0, tiles, first, 0)
-    grad_in = d_mlp_in[...]
-    scaled = grad_in * gain
-    inner = (
-        scaled
-        - jnp.mean(scaled, axis=-1, keepdims=True)
-        - normed[...] * jnp.mean(scaled * normed[...], axis=-1, keepdims=True)
-    )
+    d_up_bias[...] = jnp.zeros_like(d_up_bias)
     vectors[...] = jnp.zeros_like(vectors)
-    vectors[2:3] = jnp.sum(grad_in * normed[...], axis=0, keepdims=True)
-    vectors[3:4] = jnp.sum(grad_in, axis=0, keepdims=True)
-    for i in range(hidden_size // dmodel):
-        vectors[4 + i : 5 + i] = d_up_bias[:, i * dmodel : (i + 1) * dmodel]
-    d_branch = (cot[...].astype(jnp.float32) + inverse * inner).astype(jnp.bfloat16)
-    for t in range(tables):
-        d_branch_out[t] = d_branch[t * local_rows : (t + 1) * local_rows]
-    d_attn = lax.dot_general(d_branch, w_out[...], NT, preferred_element_type=jnp.float32).astype(jnp.bfloat16)
     width = heads * HEAD_DIM
-    for t in range(tables):
+    far_bit, group = row // groups, lax.rem(row, groups)
+    g_copies = []
+    for turn in range(tables):
+        t = lax.rem(far_bit + 1 + turn, tables)
+        mine = pl.ds(pl.multiple_of(t * local_rows, 16), local_rows)
+
+        def first(i, _):
+            at = columns(i)
+            hidden = jnp.dot(mlp_in[mine], w_up[:, at], preferred_element_type=jnp.float32) + b_up[:, at]
+            d_act = lax.dot_general(cot[mine], w_down[at], NT, preferred_element_type=jnp.float32)
+            below, slope = gelu_parts(hidden)
+            act[mine, at] = (hidden * below).astype(jnp.bfloat16)
+            grad = (d_act * (below + slope)).astype(jnp.bfloat16)
+            d_hidden[mine, at] = grad
+            d_up_bias[:, at] += jnp.sum(grad.astype(jnp.float32), axis=0, keepdims=True)
+            d_mlp_in[mine] += lax.dot_general(grad, w_up[:, at], NT, preferred_element_type=jnp.float32)
+            return 0
+
+        lax.fori_loop(0, tiles, first, 0)
+        grad_in, norm = d_mlp_in[mine], normed[mine]
+        scaled = grad_in * gain
+        inner = (
+            scaled
+            - jnp.mean(scaled, axis=-1, keepdims=True)
+            - norm * jnp.mean(scaled * norm, axis=-1, keepdims=True)
+        )
+        vectors[2:3] += jnp.sum(grad_in * norm, axis=0, keepdims=True)
+        vectors[3:4] += jnp.sum(grad_in, axis=0, keepdims=True)
+        d_branch = (cot[mine].astype(jnp.float32) + inverses[mine] * inner).astype(jnp.bfloat16)
+        d_branch_out[t] = d_branch
+        d_attn = lax.dot_general(d_branch, w_out[...], NT, preferred_element_type=jnp.float32).astype(jnp.bfloat16)
         for g in range(groups):
-            block = d_attn[t * local_rows : (t + 1) * local_rows, g * width : (g + 1) * width]
+            block = d_attn[:, g * width : (g + 1) * width]
             p = t * groups + g
             for h in range(whole):
                 packed[p, h * local_rows : (h + 1) * local_rows] = block[:, h * LANES : (h + 1) * LANES]
@@ -694,11 +698,17 @@
                 last = block[:, whole * LANES :]
                 both = jnp.concatenate([last[: local_rows // 2], last[local_rows // 2 :]], axis=1)
                 packed[p, whole * local_rows :] = both
-    own_g = pltpu.make_async_copy(packed.at[row], g_in.at[row], store_sem.at[0])
-    own_g.start()
-    g_copies = [remote(("g", k), packed.at[peer[1]], g_in.at[row], peer) for k, peer in enumerate(row_peers)]
-    for copy in g_copies:
-        copy.start()
+        for k in range(groups):
+            p = t * groups + lax.rem(group + k, groups)
+            if turn == tables - 1 and k == 0:
+                own_g = pltpu.make_async_copy(packed.at[row], g_in.at[row], store_sem.at[0])
+                own_g.start()
+            else:
+                g_copies.append(remote(("g", turn, k), packed.at[p], g_in.at[row], (tab, p)))
+                g_copies[-1].start()
+    for i in range(hidden_size // dmodel):
+        vectors[4 + i : 5 + i] = d_up_bias[:, i * dmodel : (i + 1) * dmodel]
+    d_branch = jnp.concatenate([d_branch_out[t] for t in range(tables)], axis=0)
 
     def half(ref, which):
         size = ref.shape[1] // 2
@@ -714,8 +724,13 @@
     d_mlp_in[...] = jnp.zeros_like(d_mlp_in)
     per = hidden_size // row_size
 
+    steps = row_size // 2
+
     def span_of(p):
-        return pl.ds(pl.multiple_of(p * per, LANES), per)
+        return pl.ds(pl.multiple_of(p * 2 * per, LANES), 2 * per)
+
+    def owners(p):
+        return pl.ds(2 * p, 2)
 
     def pieces(p):
         at = span_of(p)
@@ -725,7 +740,7 @@
                 device_id=core_peer, device_id_type=MESH,
             )
             for src, dst, first in (
-                (down.at[p, half(down, 1 - core)], down_in0.at[p], row_size),
+                (down.at[owners(p), half(down, 1 - core)], down_in0.at[owners(p)], row_size),
                 (up.at[:, half(up, 1 - core), at], up_in0.at[:, :, at], 2 * row_size),
             )
         ]
@@ -733,7 +748,7 @@
     def stored(p):
         at = span_of(p)
         return [
-            pltpu.make_async_copy(down_in0.at[p], down_half.at[p], store_sem.at[2 + p]),
+            pltpu.make_async_copy(down_in0.at[owners(p)], down_half.at[owners(p)], store_sem.at[2 + p]),
             pltpu.make_async_copy(up_in0.at[:, :, at], up_half.at[:, :, at], store_sem.at[2 + row_size + p]),
         ]
 
@@ -741,7 +756,8 @@
         at = span_of(p)
         for copy in pieces(p):
             copy.wait()
-        down_in0[p] = down_in0[p] + down[p, half(down, core)]
+        for q in range(2):
+            down_in0[2 * p + q] = down_in0[2 * p + q] + down[2 * p + q, half(down, core)]
         for q in range(row_size):
             up_in0[q, :, at] = up_in0[q, :, at] + up[q, half(up, core), at]
         for store in stored(p):
@@ -750,7 +766,9 @@
     def second(p, _):
         at = span_of(p)
         piece = act[:, at]
-        down[p] = jnp.dot(piece.T, cot[...], preferred_element_type=jnp.float32).astype(jnp.bfloat16)
+        d_down = jnp.dot(piece.T, cot[...], preferred_element_type=jnp.float32).astype(jnp.bfloat16)
+        for q in range(2):
+            down[2 * p + q] = d_down[q * per : (q + 1) * per]
         d_up = jnp.dot(mlp_in_t[...], d_hidden[:, at], preferred_element_type=jnp.float32).astype(jnp.bfloat16)
         for q in range(row_size):
             up[q, :, at] = d_up[q * shard : (q + 1) * shard]
@@ -764,8 +782,8 @@
 
         return 0
 
-    lax.fori_loop(0, row_size, second, 0)
-    add_piece(row_size - 1)
+    lax.fori_loop(0, steps, second, 0)
+    add_piece(steps - 1)
     out_copy.wait()
 
     @pl.loop(0, row_size)
@@ -788,7 +806,7 @@
     for i, part in enumerate(parts):
         total = jnp.where(lane == i, part, total)
     sums[...] = total
-    for p in range(row_size):
+    for p in range(steps):
         for store in stored(p):
             store.wait()
     out_store.wait()
@@ -823,7 +841,7 @@
         scratch_shapes=[
             bf16(*w_out.shape), bf16(*w_up.shape), bf16(*w_down.shape), bf16(*out_in.shape), bf16(rows, dmodel),
             bf16(rows, dmodel), bf16(rows, dmodel), bf16(dmodel, rows),
-            f32(rows, dmodel), f32(rows, dmodel), f32(rows, dmodel),
+            f32(rows, dmodel), f32(rows, dmodel), f32(rows, 1), f32(rows, dmodel),
             bf16(rows, hidden_size), bf16(rows, hidden_size), f32(1, hidden_size),
             bf16(*out_in.shape),
             bf16(row_size, shard, hidden_size), bf16(row_size, per, dmodel), bf16(row_size, shard, dmodel),
@@ -1506,7 +1524,7 @@
         qry_cot,
         groups,
         heads,
-        math.gcd(w_up.shape[1], 512),
+        math.gcd(w_up.shape[1], 1024),
         1,
     )
     ctx_feat_grad, qry_feat_grad, grad_w_emb, own, qkv_all, out_all, up_all, down_all = back(

time: 195 us -> 192 us (0.985)
  Pallas kernels: 192 us -> 188 us
    pallas_call x1, Pallas kernels: 44.9 us -> 41.1 us  [middle(): pl.pallas_call(functools.partial(middle_kernel, (row_size, ctx_rows, loca...]
where the time goes in v3:
time: 192 us; the launch traced here: 189 us
  Pallas kernels  188 us (98%)
    pallas_call x1, Pallas kernels, back(): pl.pallas_call(functools.partial(back_kernel, (row_size, x_size, chunk, c...  94.3 us
    pallas_call x1, Pallas kernels, front(): pl.pallas_call(functools.partial(front_kernel, (row_size, x_size, chunk,...  48 us
    pallas_call x1, Pallas kernels, middle(): pl.pallas_call(functools.partial(middle_kernel, (row_size, ctx_rows, loca...  41.1 us
    pallas_call x1, Pallas kernels, finish(): pl.pallas_call(kernel, out_shape=[jax.ShapeDtypeStruct((size,), jnp.float...  4.85 us

profile of v3, /device:TPU:8, one launch (start us, length us, event | category | flops | bytes accessed | tf_op | source)
XLA Modules:
  0.0 189.1 jit_solution(12096002668100393351)
XLA Ops:
  0.6 48.0 %front.1 = (bf16[8,480,128]{2,1,0:T(8,128)(2,1)}, bf16[3,2560,128]{2,1,0:T(8,128)(2,1)}, bf16[3,2048,128]{2,1,0:T(8,128)(2,1)}, bf16[3,2048,128]{2,1,0:T(8,128)(...) custom-call(s32[2]{0:T(128)} %counts.3, ...), custom_call_target="tpu_custom_call" | custom-call | tf_op jit(solution)/shard_map/front/pallas_call | solution.py:547
  48.6 41.1 %middle.1 = (bf16[2,256,768]{2,1,0:T(8,128)(2,1)}, bf16[2,64,768]{2,1,0:T(8,128)(2,1)}, bf16[8,480,128]{2,1,0:T(8,128)(2,1)}, bf16[8,48,3072]{2,1,0:T(8,128)(2,1...) custom-call(s32[2]{0:T(128)} %ctx_count.1, ...), custom_call_target="tpu_custom_call" | custom-call | tf_op jit(solution)/shard_map/middle/pallas_call | solution.py:833
  89.7 94.3 %back.1 = (bf16[100,2,256]{2,1,0:T(2,128)(2,1)}, bf16[2,64,100]{2,1,0:T(8,128)(2,1)}, f32[100,768]{1,0:T(8,128)}, f32[8,384]{1,0:T(8,128)}, bf16[96,2304]{1,0:T(...) custom-call(s32[2]{0:T(128)} %counts.3, ...), custom_call_target="tpu_custom_call" | custom-call | tf_op jit(solution)/shard_map/back/pallas_call | solution.py:1401
  184.0 4.8 %finish.1 = (f32[96]{0:T(128)}, f32[96]{0:T(128)}, f32[96]{0:T(128)}, f32[96]{0:T(128)}, f32[384]{0:T(512)}, /*index=5*/f32[4]{0:T(128)}, bf16[2,256,768]{2,1,0:...) custom-call(f32[8,384]{1,0:T(8,128)} %get-tuple-element.74.own_ref, ...), custom_call_target="tpu_custom_call" | custom-call | tf_op jit(solution)/shard_map/finish/pallas_call | solution.py:1453
